TPU v7x, 512 devices: a whole 4x8x8 slice. The times are simulated.
512 devices in a mesh: dom: 64 (over y_hi, z, core), blk: 8 (over x, y_lo).
Axes of the slice: x: 4, y: 8 (y_hi: 4, y_lo: 2; y = y_hi * 2 + y_lo), z: 8, core: 2. Of those that a mesh axis runs over, the one named last changes fastest.
Arguments:
- features: bfloat16 [65536, 128], P(('dom', 'blk')), may hold values from -6 to 6
- weight: bfloat16 [128, 256], replicated, may hold values from -0.5 to 0.5
- out_bias: float32 [256], replicated, may hold values from -4 to 4
- degree: int32 [65536], P(('dom', 'blk')), may hold values from 1 to 64
- edge_dst: int32 [512, 8, 384], P('dom', 'blk'), may hold values from 0 to 128, as said below
- edge_src: int32 [512, 8, 384], P('dom', 'blk'), may hold values from 0 to 127
- hub_rows: int32 [64, 8, 64, 64], P('dom', 'blk'), may hold values from 0 to 127
- hub_count: int32 [64, 8, 64], P('dom', 'blk'), may hold values from 1 to 64, as said below
- hub_target: int32 [64, 8, 64, 64], P('dom', 'blk'), may hold values from 0 to 127
- cotangent: bfloat16 [65536, 256], P(('dom', 'blk')), may hold values from -6 to 6
Outputs:
- activated: bfloat16 [65536, 256], P(('dom', 'blk'))
- grad_features: bfloat16 [65536, 128], P(('dom', 'blk'))
- grad_weight: float32 [128, 256], replicated
- grad_bias: float32 [256], replicated
Inputs may be any that keep to these rules, and one draw needn't show every extreme that they name: `edge_dst`: each list ends in 1 to 192 padding entries equal to 128; all other entries are below 128. `hub_count`: for every source partition and member, some destination partition receives all 64 slots.
All inputs are finite; a program needn't handle non-finite values.
Results may differ from a plain program's by a relative error of at most 0.0085.
Values may be sent and summed in bfloat16 or wider, within the bound.
A program may use at most 64 MiB of HBM per device.

v0:
```python
import jax
import jax.numpy as jnp
from jax import lax
from jax.sharding import PartitionSpec as P

TILE = 128


def build_tile(dst_lists, src_lists):
    row_blocks, col_blocks, entries = dst_lists.shape
    positions = jnp.arange(TILE, dtype=jnp.int32)

    def one_block(pair):
        dst_one, src_one = pair
        dst_hot = (dst_one[:, None] == positions[None, :]).astype(jnp.bfloat16)
        src_hot = (src_one[:, None] == positions[None, :]).astype(jnp.bfloat16)
        block_counts = lax.dot_general(
            dst_hot, src_hot, (((0,), (0,)), ((), ())), preferred_element_type=jnp.float32
        )
        return block_counts.astype(jnp.bfloat16)

    blocks = lax.map(
        one_block, (dst_lists.reshape(-1, entries), src_lists.reshape(-1, entries)), batch_size=8
    )
    blocks = blocks.reshape(row_blocks, col_blocks, TILE, TILE).transpose(0, 2, 1, 3)
    return blocks.reshape(row_blocks * TILE, col_blocks * TILE)


def source_side(came, weight, features, row_scale, send_rows, live_slots):
    width = weight.shape[1]
    in_width = weight.shape[0]
    slot_grads = lax.dot_general(
        came.reshape(-1, width),
        weight,
        (((1,), (1,)), ((), ())),
        preferred_element_type=jnp.float32,
    )
    slot_grads = slot_grads.astype(jnp.bfloat16).reshape(came.shape[0], came.shape[1], in_width)
    scale_slots = row_scale[send_rows]
    weighted = jnp.where(
        live_slots[..., None], scale_slots * came.astype(jnp.float32), jnp.float32(0.0)
    )
    slot_inputs = features[send_rows].reshape(-1, in_width).astype(jnp.float32)
    hub_weight = lax.dot_general(
        slot_inputs,
        weighted.reshape(-1, width),
        (((0,), (0,)), ((), ())),
        precision=lax.Precision.HIGHEST,
        preferred_element_type=jnp.float32,
    )
    return (slot_grads, hub_weight)


def per_device(
    features,
    weight,
    out_bias,
    degree,
    edge_dst,
    edge_src,
    hub_rows,
    hub_count,
    hub_target,
    cotangent,
):
    member_rows = features.shape[0]
    width = weight.shape[1]
    in_width = weight.shape[0]
    row_scale = lax.rsqrt(degree.astype(jnp.float32))[:, None]
    projected = (row_scale * jnp.dot(features, weight, preferred_element_type=jnp.float32)).astype(
        jnp.bfloat16
    )
    tile_src = build_tile(edge_dst, edge_src)
    empty_rows = jnp.zeros((member_rows, width), jnp.float32)
    tile_rows = lax.slice_in_dim(tile_src, 0, lax.axis_size("blk") * member_rows, axis=0)
    local_sum = lax.psum_scatter(
        jnp.dot(tile_rows, projected, preferred_element_type=jnp.float32),
        "blk",
        scatter_dimension=0,
        tiled=True,
    )
    send_rows = hub_rows[0, 0]
    slot_total = hub_count[0, 0]
    targets = hub_target[0, 0]
    live_slots = jnp.arange(send_rows.shape[1], dtype=jnp.int32)[None, :] < slot_total[:, None]
    hub_slots = jnp.where(live_slots[..., None], projected[send_rows], jnp.zeros((), jnp.bfloat16))
    arrived = lax.all_to_all(hub_slots, "dom", split_axis=0, concat_axis=0, tiled=True)
    hub_sum = jax.ops.segment_sum(
        arrived.reshape(-1, width).astype(jnp.float32),
        targets.reshape(-1),
        num_segments=member_rows,
    )
    pre_act = row_scale * (local_sum + hub_sum) + out_bias[None, :]
    activated = jax.nn.silu(pre_act).astype(jnp.bfloat16)
    sigmoid_val = jax.nn.sigmoid(pre_act)
    grad_pre = cotangent.astype(jnp.float32) * sigmoid_val * (1.0 + pre_act * (1.0 - sigmoid_val))
    bias_term = jnp.sum(grad_pre, axis=0)
    back_scaled = (row_scale * grad_pre).astype(jnp.bfloat16)
    shard_rows = lax.all_gather(back_scaled, "blk", axis=0, tiled=True)
    tile_rows = lax.slice_in_dim(tile_src, 0, shard_rows.shape[0], axis=0)
    back_local = empty_rows + lax.dot_general(
        tile_rows, shard_rows, (((0,), (0,)), ((), ())), preferred_element_type=jnp.float32
    )
    grad_local = (row_scale * back_local).astype(jnp.bfloat16)
    local_input = lax.dot_general(
        grad_local, weight, (((1,), (1,)), ((), ())), preferred_element_type=jnp.float32
    )
    weight_term = lax.dot_general(
        features, grad_local, (((0,), (0,)), ((), ())), preferred_element_type=jnp.float32
    )
    reader_slots = back_scaled[targets]
    came = lax.all_to_all(reader_slots, "dom", split_axis=0, concat_axis=0, tiled=True)
    came_back, hub_weight = source_side(came, weight, features, row_scale, send_rows, live_slots)
    masked_back = jnp.where(live_slots[..., None], came_back.astype(jnp.float32), jnp.float32(0.0))
    hub_input_back = jax.ops.segment_sum(
        masked_back.reshape(-1, in_width), send_rows.reshape(-1), num_segments=member_rows
    )
    grad_features = (local_input + row_scale * hub_input_back).astype(jnp.bfloat16)
    grad_weight, grad_bias = lax.psum((weight_term + hub_weight, bias_term), ("dom", "blk"))
    return (activated, grad_features, grad_weight, grad_bias)


def solution(mesh):
    return jax.shard_map(
        per_device,
        mesh=mesh,
        in_specs=(
            P(("dom", "blk"), None),
            P(),
            P(),
            P(("dom", "blk")),
            P("dom", "blk", None),
            P("dom", "blk", None),
            P("dom", "blk", None, None),
            P("dom", "blk", None),
            P("dom", "blk", None, None),
            P(("dom", "blk"), None),
        ),
        out_specs=(P(("dom", "blk"), None), P(("dom", "blk"), None), P(), P()),
        check_vma=False,
    )
```

profile of v0, /device:TPU:1, one launch (start us, length us, event | category | flops | bytes accessed | tf_op | source)
XLA Modules:
  0.0 622.9 jit_solution(640702102010515463)
XLA Ops:
  7.2 0.7 convert_rsqrt_fusion
  7.9 0.8 compare_select_fusion.1
  8.6 0.1 reshape.116
  8.7 0.7 iota_compare_fusion.8
  9.5 0.9 fusion.18
  10.4 14.6 %gather_fusion = bf16[4096,256]{1,0:T(8,128)(2,1)S(1)} fusion(bf16[128,256]{1,0:T(8,128)(2,1)S(1)} %fusion.18, s32[4096]{0:T(1024)S(1)} %broadcast_clamp_fusion.1), kind=kCustom, calls=%fused_computation | custom fusion | bytes 4210688 | tf_op jit(solution)/shard_map/gather | solution.py:86
  25.0 1.7 broadcast_select_fusion
  26.7 17.8 %all-to-all-start = ((bf16[64,64,256]{2,1,0:T(8,128)(2,1)}), bf16[64,64,256]{2,1,0:T(8,128)(2,1)S(1)}, u32[]{:S(2)}, u32[]{:S(2)}) async-start(bf16[64,64,256]{2,1,0:T(8,128)(2,1)} %broadcast_select_fusion), calls=%async_computation.1 | async-start | bytes 4194304 | tf_op jit(solution)/shard_map/all_to_all | solution.py:87
  44.6 0.9 fusion.12
  45.5 0.7 copy-done.2
  46.2 1.3 fusion.26
  47.6 0.1 reshape.124
  47.7 68.3 %reduce-scatter.2.cloned.1.call-done = f32[128,256]{1,0:T(8,128)} async-done(((f32[1024,256]{1,0:T(8,128)}), f32[128,256]{1,0:T(8,128)}) %reduce-scatter.2.cloned.1.call-update) | async-done | bytes 131088 | tf_op jit(solution)/shard_map/reduce_scatter | solution.py:76
  116.0 24.1 %scatter_custom_fusion = f32[128,256]{1,0:T(8,128)} fusion(f32[128,256]{1,0:T(8,128)} %reduce-scatter.2.cloned.1.call-done, s32[4096]{0:T(1024)S(1)} %reshape.150, bf16[4096,256]{1,0:T(8,128)(2,1)S(1)} %bitcast.45), kind=kCustom, calls=%fused_computation.9 | custom fusion | flops 2097152 | bytes 2228224 | tf_op jit(solution)/shard_map/scatter-add | solution.py:88
  140.1 1.7 fusion.25
  141.8 0.1 multiply_convert_fusion
  141.9 16.9 %gather_fusion.1 = bf16[4096,256]{1,0:T(8,128)(2,1)} fusion(bf16[128,256]{1,0:T(8,128)(2,1)S(1)} %multiply_convert_fusion, s32[4096]{0:T(1024)S(1)} %broadcast_clamp_fusion), kind=kCustom, calls=%fused_computation.1 | custom fusion | bytes 4210688 | tf_op jit(solution)/shard_map/gather | solution.py:111
  158.8 12.8 %all-to-all-start.1 = ((bf16[64,64,256]{2,1,0:T(8,128)(2,1)}), bf16[64,64,256]{2,1,0:T(8,128)(2,1)S(1)}, u32[]{:S(2)}, u32[]{:S(2)}) async-start(bf16[64,64,256]{2,1,0:T(8,128)(2,1)} %bitcast.6), calls=%async_computation.2 | async-start | bytes 4194304 | tf_op jit(solution)/shard_map/all_to_all | solution.py:112
  171.7 24.7 %gather_fusion.3 = f32[4096]{0:T(1024)S(1)} fusion(f32[128]{0:T(128)S(1)} %convert_rsqrt_fusion, s32[4096]{0:T(1024)S(1)} %broadcast_clamp_fusion.1), kind=kCustom, calls=%fused_computation.3 | custom fusion | bytes 49152 | tf_op jit(solution)/shard_map/gather | solution.py:39
  196.4 12.1 %gather_fusion.2 = bf16[4096,128]{1,0:T(8,128)(2,1)S(1)} fusion(bf16[128,128]{1,0:T(8,128)(2,1)S(1)} %copy-done.1, s32[4096]{0:T(1024)S(1)} %broadcast_clamp_fusion.1), kind=kCustom, calls=%fused_computation.2 | custom fusion | bytes 2113536 | tf_op jit(solution)/shard_map/gather | solution.py:43
  208.6 0.1 lt.51
  208.7 0.1 reshape.158
  208.8 111.2 %psum.15 = f32[256]{0:T(256)} all-reduce(f32[256]{0:T(256)S(1)} %get-tuple-element.27), channel_id=1, replica_groups=mesh['dom'=64,'blk'=8] {'dom','blk'}, use_global_device_ids=true, to_apply=%region_5.6 | all-reduce | flops 256 | bytes 2048 | tf_op jit(solution)/shard_map/psum | solution.py:119
  320.1 24.5 %all_gather.3 = bf16[1024,256]{1,0:T(8,128)(2,1)S(1)} all-gather(bf16[128,256]{1,0:T(8,128)(2,1)S(1)} %multiply_convert_fusion), channel_id=1, replica_groups=mesh['dom'=64,'blk'=8] {'blk'}, dimensions={0}, use_global_device_ids=true | all-gather | bytes 589824 | tf_op jit(solution)/shard_map/all_gather | solution.py:99
  344.6 1.2 fusion.17
  345.8 4.6 fusion.13
  350.5 0.9 fusion.16
  351.3 3.2 fusion.1
  354.5 22.7 %scatter_custom_fusion.1 = f32[128,128]{1,0:T(8,128)S(1)} fusion(s32[4096]{0:T(1024)S(1)} %reshape.158, f32[4096,128]{1,0:T(8,128)} %fusion.1, f32[]{:T(128)} %constant.10.clone.1), kind=kCustom, calls=%fused_computation.41 | custom fusion | flops 524288 | bytes 66048 | tf_op jit(solution)/shard_map/scatter-add | solution.py:115
  377.2 0.8 fusion.19
  378.0 236.4 %all-reduce.2.cloned.1.call-done = f32[128,256]{0,1:T(8,128)} async-done(((f32[128,256]{0,1:T(8,128)}), f32[128,256]{0,1:T(8,128)}) %all-reduce.2.cloned.1.call-update) | async-done | bytes 131088 | tf_op jit(solution)/shard_map/psum | solution.py:119
  614.4 1.7 copy.17
  (29 shorter events, 0.3 us)
Async XLA Ops:
  7.2 2.3 copy-start
  26.7 17.8 %copy-start.6 = (s32[8,1,384]{2,1,0:T(1,128)S(1)}, s32[8,1,384]{2,1,0:T(1,128)}, u32[]{:S(2)}) copy-start(s32[8,1,384]{2,1,0:T(1,128)} %param.15) | copy-start | bytes 36868
  26.7 17.9 %copy-start.7 = (s32[8,1,384]{2,1,0:T(1,128)S(1)}, s32[8,1,384]{2,1,0:T(1,128)}, u32[]{:S(2)}) copy-start(s32[8,1,384]{2,1,0:T(1,128)} %param.14) | copy-start | bytes 36868
  26.7 89.3 %all-to-all-start = ((bf16[64,64,256]{2,1,0:T(8,128)(2,1)}), bf16[64,64,256]{2,1,0:T(8,128)(2,1)S(1)}, u32[]{:S(2)}, u32[]{:S(2)}) async-start(bf16[64,64,256]{2,1,0:T(8,128)(2,1)} %broadcast_select_fusion), calls=%async_computation.1 | async-start | bytes 4194304 | tf_op jit(solution)/shard_map/all_to_all | solution.py:87
  44.5 3.0 copy-start.3
  44.5 71.5 %reduce-scatter.2.cloned.1.call-start = ((), (), s32[]{:S(2)}) async-start(), calls=%async_computation.3 | async-start | bytes 1179648 | tf_op jit(solution)/shard_map/reduce_scatter | solution.py:76
  45.5 0.7 copy-start.2
  46.2 93.9 %copy-start.5 = (bf16[128,256]{1,0:T(8,128)(2,1)S(1)}, bf16[128,256]{1,0:T(8,128)(2,1)}, u32[]{:S(2)}) copy-start(bf16[128,256]{1,0:T(8,128)(2,1)} %param.19) | copy-start | bytes 196612
  46.2 93.9 %copy-start.8 = (f32[256]{0:T(256)S(1)}, f32[256]{0:T(256)}, u32[]{:S(2)}) copy-start(f32[256]{0:T(256)} %param.12) | copy-start | bytes 3076
  158.8 187.0 %all-to-all-start.1 = ((bf16[64,64,256]{2,1,0:T(8,128)(2,1)}), bf16[64,64,256]{2,1,0:T(8,128)(2,1)S(1)}, u32[]{:S(2)}, u32[]{:S(2)}) async-start(bf16[64,64,256]{2,1,0:T(8,128)(2,1)} %bitcast.6), calls=%async_computation.2 | async-start | bytes 4194304 | tf_op jit(solution)/shard_map/all_to_all | solution.py:112
  171.6 442.8 %all-reduce.2.cloned.1.call-start = ((), (), s32[]{:S(2)}) async-start(), calls=%async_computation.4 | async-start | bytes 262144 | tf_op jit(solution)/shard_map/psum | solution.py:119
  171.7 24.7 %copy-start.1 = (bf16[128,128]{1,0:T(8,128)(2,1)S(1)}, bf16[128,128]{1,0:T(8,128)(2,1)}, u32[]{:S(2)}) copy-start(bf16[128,128]{1,0:T(8,128)(2,1)} %param.10) | copy-start | bytes 98308
  196.4 12.2 %copy-start.4 = (s32[1,1,64,64]{3,2,1,0:T(8,128)S(1)}, s32[1,1,64,64]{3,2,1,0:T(8,128)}, u32[]{:S(2)}) copy-start(s32[1,1,64,64]{3,2,1,0:T(8,128)} %param.16) | copy-start | bytes 49156
Sparse Core Ops, SparseCore 0:
  48.2 67.7 reduce-scatter.1
  351.5 262.9 all-reduce.1
where the time goes:
time: 624 us; the launch traced here: 623 us
  waiting for transfers between devices  305 us (49%)
  blocking collectives  136 us (22%)
  local copies, waits for them, and re-layouts  71.2 us (11%)
  other arithmetic  52.5 us (8%)
  starting transfers between devices  30.7 us (5%)
  between operations  14.2 us (2%)
  matrix products  13.8 us (2%)
    psum x1, waiting for transfers between devices, per_device(): lax.psum((weight_term + hub_weight, bias_term), ('dom', 'blk'))  236 us
    psum x1, blocking collectives, per_device(): lax.psum((weight_term + hub_weight, bias_term), ('dom', 'blk'))  111 us
    reduce_scatter x1, waiting for transfers between devices, per_device(): lax.psum_scatter(jnp.dot(tile_rows, projected, preferred_element_type=jnp...  68.3 us
    gather x1, local copies, waits for them, and re-layouts, source_side(): scale_slots = row_scale[send_rows]  24.7 us
    all_gather x1, blocking collectives, per_device(): shard_rows = lax.all_gather(back_scaled, 'blk', axis=0, tiled=True)  24.5 us
    scatter-add x1, other arithmetic, per_device(): jax.ops.segment_sum(arrived.reshape(-1, width).astype(jnp.float32), targe...  24.1 us
    scatter-add x1, other arithmetic, per_device(): jax.ops.segment_sum(masked_back.reshape(-1, in_width), send_rows.reshape(...  22.7 us
    all_to_all x1, starting transfers between devices, per_device(): lax.all_to_all(hub_slots, 'dom', split_axis=0, concat_axis=0, tiled=True)  17.8 us
  transfers between devices with their start and end apart: 4, of which 2 were waited for; matrix products, arithmetic and copies ran while one was open for 11% of the time, Pallas kernels for 0%

commit v1 on v0

v1 whole, which is shorter than its diff:
```python
import functools

import jax
import jax.numpy as jnp
from jax import lax
from jax.experimental import pallas as pl
from jax.experimental.pallas import tpu as pltpu
from jax.sharding import PartitionSpec as P

F32 = jnp.float32
BF16 = jnp.bfloat16
NT = (((1,), (1,)), ((), ()))
YH, ZN, CN, NB = 4, 8, 2, 8
ROWS, FIN, HID, HUB, EB = 128, 128, 256, 64, 384


def iota(shape, dim):
    return lax.broadcasted_iota(jnp.int32, shape, dim)


def mod(value, size):
    return lax.rem(value + size, size)


def column(row):
    n = row.shape[1]
    wide = jnp.broadcast_to(row.astype(F32), (n, n))
    return jnp.sum(jnp.where(iota((n, n), 0) == iota((n, n), 1), wide, 0.0), axis=1, keepdims=True)


def hot(row, size):
    return (iota((size, row.shape[1]), 0) == row).astype(F32).astype(BF16)


def kernel(
    feat_ref, weight_ref, bias_ref, degree_ref, dst_ref, src_ref, rows_ref, count_ref, target_ref, cot_ref,
    act_ref, gfeat_ref, gw_ref, gb_ref,
    xall, gall, acc, counts, counts_t, psend, precv, gblk, sendtab, loctab, mid, tab,
    w1s, w1r, w2s, w2r, w3r,
    xs_send, xs_recv, gs_send, gs_recv, p_send, p_recv, q_send, q_recv,
    i1_send, i1_recv, i2_send, i2_recv, w1_send, w1_recv, w2_send, w2_recv, w3_send, w3_recv,
):
    dom = lax.axis_index("dom")
    blk = lax.axis_index("blk")
    c = lax.rem(dom, CN)
    z = lax.rem(lax.div(dom, CN), ZN)
    y = lax.div(dom, CN * ZN)

    def at(yy, zz, cc):
        return (yy * ZN + zz) * CN + cc

    def remote(src, dst, send, recv, to_dom, to_blk):
        return pltpu.make_async_remote_copy(
            src_ref=src, dst_ref=dst, send_sem=send, recv_sem=recv,
            device_id=(to_dom, to_blk), device_id_type=pl.DeviceIdType.MESH,
        )

    barrier = pltpu.get_barrier_semaphore()

    def greet(to_dom, to_blk):
        pl.semaphore_signal(barrier, inc=1, device_id=(to_dom, to_blk), device_id_type=pl.DeviceIdType.MESH)

    def greet_a(i, carry):
        a = mod(blk * CN + c + i, NB * CN)
        greet(at(y, z, lax.rem(a, CN)), lax.div(a, CN))
        return carry

    def greet_b(i, carry):
        b = mod(y * ZN + z + i, YH * ZN)
        greet(b * CN + c, blk)
        return carry

    lax.fori_loop(1, NB * CN, greet_a, 0)
    lax.fori_loop(1, YH * ZN, greet_b, 0)
    for i in range(1, YH):
        greet(at(mod(y + i, YH), z, 1 - c), blk)

    scale = lax.rsqrt(column(degree_ref[...]))
    xs = (scale * feat_ref[...].astype(F32)).astype(BF16)
    xall[dom] = xs

    live = iota((HUB, HUB), 1).astype(F32) < column(count_ref[0])
    rows = jnp.where(live, rows_ref[0, 0], ROWS)
    target = target_ref[0, 0]
    mid_tab = jnp.concatenate([rows, target], axis=1)
    loctab[...] = jnp.concatenate([target, rows], axis=1)
    for e in range(YH * ZN * CN):
        sendtab[e // 16, (e // 2) % 8, e % 2] = mid_tab[e : e + 1, :]

    pl.semaphore_wait(barrier, (NB * CN - 1) + (YH * ZN - 1) + (YH - 1))

    def block_copy(buf, send, recv, e, k, to_dom):
        return remote(buf.at[e], buf.at[e], send.at[k], recv.at[e], to_dom, blk)

    def own_sends(buf, send, recv):
        return [
            block_copy(buf, send, recv, dom, 0, at(y, mod(z + 1, ZN), c)),
            block_copy(buf, send, recv, dom, 1, at(y, mod(z - 1, ZN), c)),
            block_copy(buf, send, recv, dom, 2, at(mod(y + 1, YH), z, c)),
            block_copy(buf, send, recv, dom, 3, at(mod(y - 1, YH), z, c)),
            block_copy(buf, send, recv, dom, 4, at(mod(y + 2, YH), z, c)),
            block_copy(buf, send, recv, dom, 5, at(y, z, 1 - c)),
        ]

    def y_block(t):
        return jnp.where(t == 0, 3, t)

    def dy_of(k):
        return jnp.where(k == 0, 0, y_block(k - 1))

    def far_sign(k):
        return jnp.where(k < 2, 1, -1)

    def gather_loop(buf, send, recv, extra, forward):
        def contribution(m):
            pieces = []
            for cc in range(CN):
                e = m * CN + cc
                lanes = iota((1, 2 * HUB), 1)
                mine = jnp.where((lanes < HUB) == forward, loctab[pl.ds(e, 1), :], -1)
                theirs = tab[lax.div(m, ZN), lax.rem(m, ZN), cc]
                pieces.append(
                    lax.dot_general(hot(mine, ROWS), hot(theirs, ROWS), NT, preferred_element_type=F32).astype(BF16)
                )
            joint = jnp.concatenate(pieces, axis=1)
            return jnp.dot(joint, buf[pl.ds(m * CN, CN)].reshape(CN * ROWS, FIN), preferred_element_type=F32)

        def wait_block(e):
            block_copy(buf, send, recv, e, 0, dom).wait_recv()

        def step(t, carry):
            k = lax.rem(t, 4)
            s = lax.div(t, 4) + 1

            @pl.when(t < 3)
            def _():
                e = at(mod(y + y_block(t), YH), z, c)
                wait_block(e)
                block_copy(buf, send, recv, e, 6 + 3 * t, at(y, mod(z + 1, ZN), c)).start()
                block_copy(buf, send, recv, e, 7 + 3 * t, at(y, mod(z - 1, ZN), c)).start()
                block_copy(buf, send, recv, e, 8 + 3 * t, at(y, z, 1 - c)).start()

            @pl.when(t < 16)
            def _():
                for slot, sign in ((0, 1), (1, -1)):
                    far = far_sign(k) == sign

                    @pl.when((s < 4) | far)
                    def _():
                        e = at(mod(y + dy_of(k), YH), mod(z - sign * s, ZN), c)
                        wait_block(e)

                        @pl.when((s < 3) | ((s == 3) & far))
                        def _():
                            block_copy(buf, send, recv, e, 15 + 4 * t + slot, at(y, mod(z + sign, ZN), c)).start()

                        block_copy(buf, send, recv, e, 17 + 4 * t + slot, at(y, z, 1 - c)).start()

            extra(t)

            @pl.when(t < 4)
            def _():
                m = mod(y + dy_of(t), YH) * ZN + z
                wait_block(m * CN + 1 - c)
                acc[...] += contribution(m)

            prev = t - 1
            pk = lax.rem(prev + 4, 4)
            ps = lax.div(prev, 4) + 1
            row = mod(y + dy_of(pk), YH) * ZN

            @pl.when((t >= 1) & (t <= 12))
            def _():
                up = row + mod(z - ps, ZN)
                down = row + mod(z + ps, ZN)
                wait_block(up * CN + 1 - c)
                wait_block(down * CN + 1 - c)
                acc[...] += contribution(up) + contribution(down)

            @pl.when(t > 12)
            def _():
                m = row + mod(z + 4, ZN)
                wait_block(m * CN + 1 - c)
                acc[...] += contribution(m)

            return carry

        lax.fori_loop(0, 17, step, 0)

    def gather_finish(buf, send, recv):
        for k in range(6):
            block_copy(buf, send, recv, dom, k, dom).wait_send()

        def drain_y(t, carry):
            for i in range(3):
                block_copy(buf, send, recv, dom, 6 + 3 * t + i, dom).wait_send()
            return carry

        def drain(t, carry):
            k = lax.rem(t, 4)
            s = lax.div(t, 4) + 1
            for slot, sign in ((0, 1), (1, -1)):
                far = far_sign(k) == sign

                @pl.when((s < 3) | ((s == 3) & far))
                def _():
                    block_copy(buf, send, recv, dom, 15 + 4 * t + slot, dom).wait_send()

                @pl.when((s < 4) | far)
                def _():
                    block_copy(buf, send, recv, dom, 17 + 4 * t + slot, dom).wait_send()

            return carry

        lax.fori_loop(0, 3, drain_y, 0)
        lax.fori_loop(0, 16, drain, 0)

    for copy in own_sends(xall, xs_send, xs_recv):
        copy.start()

    def table_z(i):
        zz = mod(z + i, ZN)
        return remote(sendtab.at[:, zz], mid.at[:, :, z], i1_send.at[i], i1_recv.at[z], at(y, zz, c), blk)

    def table_z_in(i):
        zz = mod(z + i, ZN)
        return remote(sendtab.at[:, zz], mid.at[:, :, zz], i1_send.at[i], i1_recv.at[zz], at(y, zz, c), blk)

    def table_yc(i):
        other = mod(y * CN + c + i, YH * CN)
        yy, cc = lax.div(other, CN), lax.rem(other, CN)
        return remote(
            mid.at[yy, cc], tab.at[y, :, c], i2_send.at[i], i2_recv.at[y * CN + c], at(yy, z, cc), blk
        )

    def table_yc_in(i):
        other = mod(y * CN + c + i, YH * CN)
        yy, cc = lax.div(other, CN), lax.rem(other, CN)
        return remote(mid.at[yy, cc], tab.at[yy, :, cc], i2_send.at[i], i2_recv.at[other], at(yy, z, cc), blk)

    for i in range(1, ZN):
        table_z(i).start()
    for yy in range(YH):
        for cc in range(CN):
            mid[yy, cc, z] = sendtab[yy, z, cc]
    for i in range(1, ZN):
        table_z_in(i).wait_recv()
    for i in range(1, YH * CN):
        table_yc(i).start()
    for zz in range(ZN):
        tab[y, zz, c] = mid[y, c, zz]

    acc[...] = jnp.zeros_like(acc)

    def part_copy(a, to_blk, came):
        return remote(psend.at[a], precv.at[came], p_send.at[a], p_recv.at[came], dom, to_blk)

    def forward_extra(t):
        @pl.when(t < NB)
        def _():
            a = mod(blk + 1 + t, NB)
            dst_hot = hot(dst_ref[a], ROWS)
            src_hot = hot(src_ref[a], ROWS)
            count = lax.dot_general(dst_hot, src_hot, NT, preferred_element_type=F32).astype(BF16)
            count_t = lax.dot_general(src_hot, dst_hot, NT, preferred_element_type=F32).astype(BF16)
            counts_t[a] = count_t
            part = jnp.dot(count, xall[dom], preferred_element_type=F32)

            @pl.when(a != blk)
            def _():
                psend[a] = part.astype(BF16)
                part_copy(a, a, blk).start()

            @pl.when(a == blk)
            def _():
                counts[...] = part

        @pl.when(t == 0)
        def _():
            for i in range(1, YH * CN):
                table_yc_in(i).wait_recv()

    gather_loop(xall, xs_send, xs_recv, forward_extra, True)

    total = acc[...] + counts[...]
    for i in range(1, NB):
        other = mod(blk + i, NB)
        part_copy(other, other, other).wait_recv()
        total = total + precv[other].astype(F32)

    weight = weight_ref[...]
    pre = scale * jnp.dot(total.astype(BF16), weight, preferred_element_type=F32) + bias_ref[...]
    sig = jax.nn.sigmoid(pre)
    act_ref[...] = (pre * sig).astype(BF16)
    grad_pre = cot_ref[...].astype(F32) * sig * (1.0 + pre * (1.0 - sig))
    back = (scale * grad_pre).astype(BF16)
    grad = lax.dot_general(back, weight, NT, preferred_element_type=F32).astype(BF16)
    gall[dom] = grad
    for copy in own_sends(gall, gs_send, gs_recv):
        copy.start()

    gblk[blk] = grad

    def member_copy(i, came):
        other = mod(blk + i, NB)
        return remote(gall.at[dom], gblk.at[came], q_send.at[i], q_recv.at[came], dom, other)

    for i in range(1, NB):
        member_copy(i, blk).start()

    bias_term = jnp.sum(grad_pre, axis=0, keepdims=True)
    gw = jnp.dot(total.T.astype(BF16), back, preferred_element_type=F32)
    me_a = blk * CN + c
    me_b = y * ZN + z
    for a in range(NB * CN):
        w1s[a, 0:8, :] = gw[8 * a : 8 * a + 8, 0:128]
        w1s[a, 8:16, :] = gw[8 * a : 8 * a + 8, 128:256]
        w1s[a, 16:17, :] = bias_term[:, 0:128]
        w1s[a, 17:18, :] = bias_term[:, 128:256]
    w1r[me_a] = w1s[me_a]

    def w1_copy(i, incoming):
        a = mod(me_a + i, NB * CN)
        came = a if incoming else me_a
        return remote(
            w1s.at[a], w1r.at[came], w1_send.at[i], w1_recv.at[came], at(y, z, lax.rem(a, CN)), lax.div(a, CN)
        )

    def w2_copy(i, incoming):
        b = mod(me_b + i, YH * ZN)
        came = b if incoming else me_b
        return remote(w2s, w2r.at[came], w2_send.at[i], w2_recv.at[came], b * CN + c, blk)

    def w3_copy(i, incoming):
        a = mod(me_a + i, NB * CN)
        came = a if incoming else me_a
        return remote(
            w3r.at[came], w3r.at[came], w3_send.at[i], w3_recv.at[came], at(y, z, lax.rem(a, CN)), lax.div(a, CN)
        )

    def each(count, body):
        def run(i, carry):
            body(i)
            return carry

        lax.fori_loop(1, count, run, 0)

    each(NB * CN, lambda i: w1_copy(i, False).start())

    acc[...] = jnp.zeros_like(acc)

    def backward_extra(t):
        @pl.when(t == 3)
        def _():
            each(NB * CN, lambda i: w1_copy(i, True).wait_recv())
            w2s[...] = jnp.sum(w1r[...], axis=0)
            w2r[me_b] = w2s[...]
            each(YH * ZN, lambda i: w2_copy(i, False).start())

        @pl.when(t == 9)
        def _():
            each(YH * ZN, lambda i: w2_copy(i, True).wait_recv())
            w3r[me_a] = jnp.sum(w2r[...], axis=0)
            each(NB * CN, lambda i: w3_copy(i, False).start())

    gather_loop(gall, gs_send, gs_recv, backward_extra, False)

    total_back = acc[...]
    for i in range(1, NB):
        member_copy(i, mod(blk + i, NB)).wait_recv()
    for a in range(NB):
        total_back = total_back + jnp.dot(counts_t[a], gblk[a], preferred_element_type=F32)
    gfeat_ref[...] = (scale * total_back).astype(BF16)

    each(NB * CN, lambda i: w3_copy(i, True).wait_recv())
    for a in range(NB * CN):
        gw_ref[8 * a : 8 * a + 8, 0:128] = w3r[a, 0:8, :]
        gw_ref[8 * a : 8 * a + 8, 128:256] = w3r[a, 8:16, :]
    gb_ref[...] = w3r[me_a, 16:18, :]

    gather_finish(xall, xs_send, xs_recv)
    gather_finish(gall, gs_send, gs_recv)
    for i in range(1, ZN):
        table_z(i).wait_send()
    for i in range(1, YH * CN):
        table_yc(i).wait_send()
    for i in range(1, NB):
        other = mod(blk + i, NB)
        part_copy(other, other, blk).wait_send()
        member_copy(i, blk).wait_send()
    each(NB * CN, lambda i: w1_copy(i, False).wait_send())
    each(YH * ZN, lambda i: w2_copy(i, False).wait_send())
    each(NB * CN, lambda i: w3_copy(i, False).wait_send())


def per_device(features, weight, out_bias, degree, edge_dst, edge_src, hub_rows, hub_count, hub_target, cotangent):
    nd = YH * ZN * CN
    vmem = pl.BlockSpec(memory_space=pltpu.VMEM)
    dma = pltpu.SemaphoreType.DMA
    act, gfeat, gw, gb = pl.pallas_call(
        kernel,
        out_shape=(
            jax.ShapeDtypeStruct((ROWS, HID), BF16),
            jax.ShapeDtypeStruct((ROWS, FIN), BF16),
            jax.ShapeDtypeStruct((FIN, HID), F32),
            jax.ShapeDtypeStruct((2, 128), F32),
        ),
        in_specs=[vmem] * 10,
        out_specs=(vmem,) * 4,
        scratch_shapes=[
            pltpu.VMEM((nd, ROWS, FIN), BF16),
            pltpu.VMEM((nd, ROWS, FIN), BF16),
            pltpu.VMEM((ROWS, FIN), F32),
            pltpu.VMEM((ROWS, FIN), F32),
            pltpu.VMEM((NB, ROWS, ROWS), BF16),
            pltpu.VMEM((NB, ROWS, FIN), BF16),
            pltpu.VMEM((NB, ROWS, FIN), BF16),
            pltpu.VMEM((NB, ROWS, FIN), BF16),
            pltpu.VMEM((YH, ZN, CN, 1, 2 * HUB), jnp.int32),
            pltpu.VMEM((nd, 2 * HUB), jnp.int32),
            pltpu.VMEM((YH, CN, ZN, 1, 2 * HUB), jnp.int32),
            pltpu.VMEM((YH, ZN, CN, 1, 2 * HUB), jnp.int32),
            pltpu.VMEM((NB * CN, 18, 128), F32),
            pltpu.VMEM((NB * CN, 18, 128), F32),
            pltpu.VMEM((18, 128), F32),
            pltpu.VMEM((YH * ZN, 18, 128), F32),
            pltpu.VMEM((NB * CN, 18, 128), F32),
            dma((80,)), dma((nd,)), dma((80,)), dma((nd,)),
            dma((NB,)), dma((NB,)), dma((NB,)), dma((NB,)),
            dma((ZN,)), dma((ZN,)), dma((YH * CN,)), dma((YH * CN,)),
            dma((NB * CN,)), dma((NB * CN,)), dma((YH * ZN,)), dma((YH * ZN,)), dma((NB * CN,)), dma((NB * CN,)),
        ],
        compiler_params=pltpu.CompilerParams(
            collective_id=0, has_side_effects=True, vmem_limit_bytes=24 * 1024 * 1024
        ),
    )(
        features, weight, out_bias.reshape(1, HID), degree.reshape(1, ROWS), edge_dst, edge_src,
        hub_rows, hub_count, hub_target, cotangent,
    )
    return act, gfeat, gw, gb.reshape(HID)


def solution(mesh):
    return jax.shard_map(
        per_device,
        mesh=mesh,
        in_specs=(
            P(("dom", "blk"), None),
            P(),
            P(),
            P(("dom", "blk")),
            P("dom", "blk", None),
            P("dom", "blk", None),
            P("dom", "blk", None, None),
            P("dom", "blk", None),
            P("dom", "blk", None, None),
            P(("dom", "blk"), None),
        ),
        out_specs=(P(("dom", "blk"), None), P(("dom", "blk"), None), P(), P()),
        check_vma=False,
    )
```

time: 624 us -> 87.8 us (0.14)
  waiting for transfers between devices: 305 us -> 0 us
  blocking collectives: 136 us -> 0 us
  Pallas kernels: 0 us -> 78.1 us
  local copies, waits for them, and re-layouts: 71.2 us -> 8.5 us
  other arithmetic: 52.5 us -> 0 us
  starting transfers between devices: 30.7 us -> 0 us
  matrix products: 13.8 us -> 0 us
  between operations: 14.2 us -> 0.68 us
    psum x1 -> x0, waiting for transfers between devices: 236 us -> none  [per_device(): lax.psum((weight_term + hub_weight, bias_term), ('dom', 'blk'))]
    psum x1 -> x0, blocking collectives: 111 us -> none  [per_device(): lax.psum((weight_term + hub_weight, bias_term), ('dom', 'blk'))]
    pallas_call x0 -> x1, Pallas kernels: none -> 78.1 us  [per_device(): pl.pallas_call(kernel, out_shape=(jax.ShapeDtypeStruct((ROWS, HID), BF16)...]
    gather x4 -> x0, local copies, waits for them, and re-layouts: 68.4 us -> none  [the longest x1 24.7 us: source_side(): scale_slots = row_scale[send_rows]]
    reduce_scatter x1 -> x0, waiting for transfers between devices: 68.3 us -> none  [per_device(): lax.psum_scatter(jnp.dot(tile_rows, projected, preferred_element_type=jnp...]
    scatter-add x2 -> x0, other arithmetic: 46.8 us -> none  [the longest x1 24.1 us: per_device(): jax.ops.segment_sum(arrived.reshape(-1, width).astype(jnp.float32), targe...]
    all_to_all x2 -> x0, starting transfers between devices: 30.6 us -> none  [the longest x1 17.8 us: per_device(): lax.all_to_all(hub_slots, 'dom', split_axis=0, concat_axis=0, tiled=True)]
    all_gather x1 -> x0, blocking collectives: 24.5 us -> none  [per_device(): shard_rows = lax.all_gather(back_scaled, 'blk', axis=0, tiled=True)]
  transfers between devices with their start and end apart: 4 -> 0, of which waited for: 2 -> 0; matrix products, arithmetic and copies ran while one was open for 11% -> 0% of each run, Pallas kernels for 0% -> 0%
where the time goes in v1:
time: 87.8 us; the launch traced here: 87.3 us
  Pallas kernels  78.1 us (89%)
  local copies, waits for them, and re-layouts  8.5 us (10%)
    pallas_call x1, Pallas kernels, per_device(): pl.pallas_call(kernel, out_shape=(jax.ShapeDtypeStruct((ROWS, HID), BF16)...  78.1 us
    unnamed x24, local copies, waits for them, and re-layouts  8.5 us

profile of v1, /device:TPU:1, one launch (start us, length us, event | category | flops | bytes accessed | tf_op | source)
XLA Modules:
  0.0 87.3 jit_solution(6969057665013703928)
XLA Ops:
  0.6 0.0 copy-start.9
  0.6 0.0 copy-start.7
  0.7 0.0 copy-start.8
  0.7 0.6 copy-done.9
  1.3 0.0 copy-done.7
  1.3 0.0 copy-done.8
  1.3 0.0 copy-start
  1.3 0.8 copy-done
  2.2 0.0 copy-start.1
  2.2 0.8 copy-done.1
  3.0 0.0 copy-start.2
  3.0 0.8 copy-done.2
  3.8 0.0 copy-start.3
  3.8 0.8 copy-done.3
  4.5 0.0 copy-start.4
  4.5 0.8 copy-done.4
  5.3 0.0 copy-start.5
  5.3 0.7 copy-done.5
  6.0 0.0 copy-start.6
  6.0 0.7 copy-done.6
  6.7 78.1 %shard_map.129 = (bf16[128,256]{1,0:T(8,128)(2,1)S(1)}, bf16[128,128]{1,0:T(8,128)(2,1)S(1)}, f32[128,256]{1,0:T(8,128)S(1)}, f32[2,128]{1,0:T(2,128)S(1)}) custom-call(bf16[128,128]{1,0:T(8,128)(2,1)S(1)} %copy-done.2, bf16[128,256]{1,0:T(8,128)(2,1)S(1)} %copy-done, f32[1,256]{1,0:T(1,128)S(1)} %bitcast.3, s32[1,128]{1,0:T(1,128)S(1)} %bitcast.5, ...), custom_call_target="tpu_custom_call" | custom-call | tf_op jit(solution)/shard_map/pallas_call | solution.py:400
  84.8 0.6 copy.18
  85.4 0.6 copy.19
  86.0 0.7 copy.20
  86.7 0.6 copy.21
Async XLA Ops:
  0.6 0.7 copy-start.9
  0.6 0.7 copy-start.7
  0.7 0.7 copy-start.8
  1.3 0.8 copy-start
  2.2 0.8 copy-start.1
  3.0 0.8 copy-start.2
  3.8 0.8 copy-start.3
  4.5 0.8 copy-start.4
  5.3 0.7 copy-start.5
  6.0 0.7 copy-start.6

commit v2 on v1

v2 whole, which is shorter than its diff:
```python
import functools

import jax
import jax.numpy as jnp
from jax import lax
from jax.experimental import pallas as pl
from jax.experimental.pallas import tpu as pltpu
from jax.sharding import PartitionSpec as P

F32 = jnp.float32
BF16 = jnp.bfloat16
NT = (((1,), (1,)), ((), ()))
YH, ZN, CN, NB = 4, 8, 2, 8
ROWS, FIN, HID, HUB, EB = 128, 128, 256, 64, 384


def iota(shape, dim):
    return lax.broadcasted_iota(jnp.int32, shape, dim)


def mod(value, size):
    return lax.rem(value + size, size)


def column(row):
    n = row.shape[1]
    wide = jnp.broadcast_to(row.astype(F32), (n, n))
    return jnp.sum(jnp.where(iota((n, n), 0) == iota((n, n), 1), wide, 0.0), axis=1, keepdims=True)


def hot(row, size):
    return (iota((size, row.shape[1]), 0) == row).astype(F32).astype(BF16)


def kernel(
    feat_hbm, weight_hbm, bias_hbm, degree_hbm, dst_hbm, src_hbm, rows_hbm, count_hbm, target_hbm, cot_hbm,
    act_hbm, gfeat_hbm, gw_hbm, gb_hbm,
    feat_ref, weight_ref, bias_ref, degree_ref, dst_ref, src_ref, rows_ref, count_ref, target_ref, cot_ref,
    act_ref, gfeat_ref, gw_ref, gb_ref,
    xall, gall, acc, own_part, counts_t, psend, precv, gblk, sendtab, loctab, mid, tab,
    w1s, w1r, w2r, w3r, w4r,
    in_sem, out_sem, xs_send, xs_recv, gs_send, gs_recv, p_send, p_recv, q_send, q_recv,
    i1_send, i1_recv, i2_send, i2_recv, w_send, w_recv,
):
    dom = lax.axis_index("dom")
    blk = lax.axis_index("blk")
    c = lax.rem(dom, CN)
    z = lax.rem(lax.div(dom, CN), ZN)
    y = lax.div(dom, CN * ZN)

    def at(yy, zz, cc):
        return (yy * ZN + zz) * CN + cc

    def each(count, body):
        def run(i, carry):
            body(i)
            return carry

        lax.fori_loop(1, count, run, 0)

    barrier = pltpu.get_barrier_semaphore()

    def greet(to_dom, to_blk):
        pl.semaphore_signal(barrier, inc=1, device_id=(to_dom, to_blk), device_id_type=pl.DeviceIdType.MESH)

    def greet_a(i):
        a = mod(blk * CN + c + i, NB * CN)
        greet(at(y, z, lax.rem(a, CN)), lax.div(a, CN))

    def greet_y(i):
        other = mod(y * CN + c + i, YH * CN)
        greet(at(lax.div(other, CN), z, lax.rem(other, CN)), blk)

    for i in range(1, ZN):
        greet(at(y, mod(z + i, ZN), c), blk)
    for i in range(1, YH):
        greet(at(mod(y + i, YH), z, c), blk)
        greet(at(mod(y + i, YH), z, 1 - c), blk)
    each(NB * CN, greet_a)

    incoming = [
        pltpu.make_async_copy(src, dst, in_sem.at[i])
        for i, (src, dst) in enumerate(
            (
                (degree_hbm, degree_ref), (feat_hbm, feat_ref), (count_hbm.at[0], count_ref),
                (rows_hbm.at[0, 0], rows_ref), (target_hbm.at[0, 0], target_ref), (dst_hbm, dst_ref),
                (src_hbm, src_ref), (weight_hbm, weight_ref), (bias_hbm, bias_ref), (cot_hbm, cot_ref),
            )
        )
    ]
    for copy in incoming:
        copy.start()

    outgoing = [
        pltpu.make_async_copy(src, dst, out_sem.at[i])
        for i, (src, dst) in enumerate(
            ((act_ref, act_hbm), (gfeat_ref, gfeat_hbm), (gw_ref, gw_hbm), (gb_ref, gb_hbm))
        )
    ]

    def remote(src, dst, send, recv, to_dom, to_blk):
        return pltpu.make_async_remote_copy(
            src_ref=src, dst_ref=dst, send_sem=send, recv_sem=recv,
            device_id=(to_dom, to_blk), device_id_type=pl.DeviceIdType.MESH,
        )

    def taken(ref, send, recv):
        return remote(ref, ref, send, recv, dom, blk)

    incoming[0].wait()
    incoming[1].wait()
    scale = lax.rsqrt(column(degree_ref[...]))
    xs = (scale * feat_ref[...].astype(F32)).astype(BF16)
    xall[dom] = xs

    pl.semaphore_wait(barrier, (NB * CN - 1) + (ZN - 1) + 2 * (YH - 1))

    def block_copy(buf, send, recv, e, to_dom):
        return remote(buf.at[e], buf.at[e], send, recv.at[e], to_dom, blk)

    def own_sends(buf, send, recv):
        for to_dom in (
            at(y, mod(z + 1, ZN), c), at(y, mod(z - 1, ZN), c),
            at(mod(y - 1, YH), z, c), at(mod(y + 1, YH), z, c), at(mod(y + 2, YH), z, c),
            at(y, z, 1 - c),
        ):
            block_copy(buf, send, recv, dom, to_dom).start()

    def y_block(t):
        return jnp.where(t == 0, 1, jnp.where(t == 1, 3, 2))

    def dy_of(k):
        return jnp.where(k == 0, 0, y_block(k - 1))

    def far_sign(k):
        return jnp.where(k < 2, 1, -1)

    def gather_loop(buf, send, recv, extra, forward):
        def contribution(m):
            pieces = []
            for cc in range(CN):
                e = m * CN + cc
                lanes = iota((1, 2 * HUB), 1)
                mine = jnp.where((lanes < HUB) == forward, loctab[pl.ds(e, 1), :], -1)
                theirs = tab[lax.rem(m, ZN), lax.div(m, ZN) * CN + cc]
                pieces.append(
                    lax.dot_general(hot(mine, ROWS), hot(theirs, ROWS), NT, preferred_element_type=F32).astype(BF16)
                )
            joint = jnp.concatenate(pieces, axis=1)
            return jnp.dot(joint, buf[pl.ds(m * CN, CN)].reshape(CN * ROWS, FIN), preferred_element_type=F32)

        def wait_block(e):
            block_copy(buf, send, recv, e, dom).wait_recv()

        def group(g, carry):
            k = lax.rem(g, 4)
            s = lax.div(g, 4) + 1
            row = mod(y + dy_of(k), YH) * ZN

            @pl.when(g < 4)
            def _():
                wait_block((row + z) * CN + 1 - c)
                acc[...] += contribution(row + z)

            @pl.when(g < 12)
            def _():
                up = row + mod(z - s, ZN)
                down = row + mod(z + s, ZN)
                wait_block(up * CN + 1 - c)
                wait_block(down * CN + 1 - c)
                acc[...] += contribution(up) + contribution(down)

            @pl.when(g >= 12)
            def _():
                m = row + mod(z + 4, ZN)
                wait_block(m * CN + 1 - c)
                acc[...] += contribution(m)

            return carry

        def step(t, low):
            k = lax.rem(t, 4)
            s = lax.div(t, 4) + 1

            @pl.when(t < 3)
            def _():
                e = at(mod(y + y_block(t), YH), z, c)
                wait_block(e)
                block_copy(buf, send, recv, e, at(y, mod(z + 1, ZN), c)).start()
                block_copy(buf, send, recv, e, at(y, mod(z - 1, ZN), c)).start()
                block_copy(buf, send, recv, e, at(y, z, 1 - c)).start()

            @pl.when(t < 16)
            def _():
                for sign in (1, -1):
                    far = far_sign(k) == sign

                    @pl.when((s < 4) | far)
                    def _():
                        e = at(mod(y + dy_of(k), YH), mod(z - sign * s, ZN), c)
                        wait_block(e)

                        @pl.when((s < 3) | ((s == 3) & far))
                        def _():
                            block_copy(buf, send, recv, e, at(y, mod(z + sign, ZN), c)).start()

                        block_copy(buf, send, recv, e, at(y, z, 1 - c)).start()

            extra(t)
            if forward:
                high = jnp.where(t < 5, 0, jnp.minimum(2 * (t - 4), t))
            else:
                high = t
            lax.fori_loop(low, high, group, 0)
            return high

        lax.fori_loop(0, 17, step, 0)
        taken(buf.at[pl.ds(0, YH * ZN * CN - 1)], send, recv.at[0]).wait_send()

    own_sends(xall, xs_send, xs_recv)

    incoming[2].wait()
    incoming[3].wait()
    incoming[4].wait()
    live = iota((HUB, HUB), 1).astype(F32) < column(count_ref[...])
    rows = jnp.where(live, rows_ref[...], ROWS)
    target = target_ref[...]
    joint_tab = jnp.concatenate([rows, target], axis=1)
    loctab[...] = jnp.concatenate([target, rows], axis=1)
    for e in range(YH * ZN * CN):
        sendtab[(e // CN) % ZN, (e // (CN * ZN)) * CN + e % CN] = joint_tab[e : e + 1, :]

    def table_z(i):
        zz = mod(z + i, ZN)
        return remote(sendtab.at[zz], mid.at[z], i1_send, i1_recv, at(y, zz, c), blk)

    def table_yc(i):
        other = mod(y * CN + c + i, YH * CN)
        to_dom = at(lax.div(other, CN), z, lax.rem(other, CN))
        return remote(mid.at[:, other], tab.at[:, y * CN + c], i2_send, i2_recv, to_dom, blk)

    each(ZN, lambda i: table_z(i).start())
    mid[z] = sendtab[z]
    acc[...] = jnp.zeros_like(acc)
    incoming[5].wait()
    incoming[6].wait()

    def part_copy(a):
        return remote(psend.at[a], precv.at[blk], p_send, p_recv, dom, a)

    def forward_extra(t):
        @pl.when(t == 1)
        def _():
            taken(mid.at[pl.ds(0, ZN - 1)], i1_send, i1_recv).wait_recv()
            each(YH * CN, lambda i: table_yc(i).start())
            tab[:, y * CN + c] = mid[:, y * CN + c]

        @pl.when(t < NB)
        def _():
            a = mod(blk + 1 + t, NB)
            dst_hot = hot(dst_ref[a], ROWS)
            src_hot = hot(src_ref[a], ROWS)
            count = lax.dot_general(dst_hot, src_hot, NT, preferred_element_type=F32).astype(BF16)
            count_t = lax.dot_general(src_hot, dst_hot, NT, preferred_element_type=F32).astype(BF16)
            counts_t[a] = count_t
            part = jnp.dot(count, xall[dom], preferred_element_type=F32)

            @pl.when(a != blk)
            def _():
                psend[a] = part.astype(BF16)
                part_copy(a).start()

            @pl.when(a == blk)
            def _():
                own_part[...] = part
                precv[blk] = jnp.zeros((ROWS, FIN), BF16)

        @pl.when(t == 5)
        def _():
            taken(tab.at[pl.ds(0, YH * CN - 1)], i2_send, i2_recv).wait_recv()

        @pl.when(t == 14)
        def _():
            taken(precv.at[pl.ds(0, NB - 1)], p_send, p_recv).wait_recv()
            part = own_part[...]
            for i in range(NB):
                part = part + precv[i].astype(F32)
            acc[...] += part

    gather_loop(xall, xs_send, xs_recv, forward_extra, True)

    for i in (7, 8, 9):
        incoming[i].wait()
    total = acc[...]
    weight = weight_ref[...]
    pre = scale * jnp.dot(total.astype(BF16), weight, preferred_element_type=F32) + bias_ref[...]
    sig = jax.nn.sigmoid(pre)
    grad_pre = cot_ref[...].astype(F32) * sig * (1.0 + pre * (1.0 - sig))
    back = (scale * grad_pre).astype(BF16)
    grad = lax.dot_general(back, weight, NT, preferred_element_type=F32).astype(BF16)
    gall[dom] = grad
    own_sends(gall, gs_send, gs_recv)
    gblk[blk] = grad

    def member_copy(i):
        return remote(gall.at[dom], gblk.at[blk], q_send, q_recv, dom, mod(blk + i, NB))

    each(NB, lambda i: member_copy(i).start())

    act_ref[...] = (pre * sig).astype(BF16)
    outgoing[0].start()
    bias_term = jnp.sum(grad_pre, axis=0, keepdims=True)
    gw = jnp.dot(total.T.astype(BF16), back, preferred_element_type=F32)
    me_a = blk * CN + c
    for a in range(NB * CN):
        w1s[a, 0:8, :] = gw[8 * a : 8 * a + 8, 0:128]
        w1s[a, 8:16, :] = gw[8 * a : 8 * a + 8, 128:256]
        w1s[a, 16:17, :] = bias_term[:, 0:128]
        w1s[a, 17:18, :] = bias_term[:, 128:256]
    w1r[me_a] = w1s[me_a]

    def w1_copy(i):
        a = mod(me_a + i, NB * CN)
        return remote(
            w1s.at[a], w1r.at[me_a], w_send.at[0], w_recv.at[0], at(y, z, lax.rem(a, CN)), lax.div(a, CN)
        )

    def w2_copy(i):
        return remote(w2r.at[y], w2r.at[y], w_send.at[1], w_recv.at[1], at(mod(y + i, YH), z, c), blk)

    def w3_copy(i):
        return remote(w3r.at[z], w3r.at[z], w_send.at[2], w_recv.at[2], at(y, mod(z + i, ZN), c), blk)

    def w4_copy(i):
        a = mod(me_a + i, NB * CN)
        return remote(
            w4r.at[me_a], w4r.at[me_a], w_send.at[3], w_recv.at[3], at(y, z, lax.rem(a, CN)), lax.div(a, CN)
        )

    def others(ref, count, which):
        return taken(ref.at[pl.ds(0, count - 1)], w_send.at[which], w_recv.at[which])

    each(NB * CN, lambda i: w1_copy(i).start())

    acc[...] = jnp.zeros_like(acc)

    def backward_extra(t):
        @pl.when(t == 4)
        def _():
            others(w1r, NB * CN, 0).wait_recv()
            w2r[y] = jnp.sum(w1r[...], axis=0)
            each(YH, lambda i: w2_copy(i).start())

        @pl.when(t == 8)
        def _():
            others(w2r, YH, 1).wait_recv()
            w3r[z] = jnp.sum(w2r[...], axis=0)
            each(ZN, lambda i: w3_copy(i).start())

        @pl.when(t == 12)
        def _():
            others(w3r, ZN, 2).wait_recv()
            w4r[me_a] = jnp.sum(w3r[...], axis=0)
            each(NB * CN, lambda i: w4_copy(i).start())

        @pl.when(t == 14)
        def _():
            taken(gblk.at[pl.ds(0, NB - 1)], q_send, q_recv).wait_recv()
            total_back = acc[...]
            for a in range(NB):
                total_back = total_back + jnp.dot(counts_t[a], gblk[a], preferred_element_type=F32)
            acc[...] = total_back

    gather_loop(gall, gs_send, gs_recv, backward_extra, False)

    gfeat_ref[...] = (scale * acc[...]).astype(BF16)
    outgoing[1].start()
    others(w4r, NB * CN, 3).wait_recv()
    for a in range(NB * CN):
        gw_ref[8 * a : 8 * a + 8, 0:128] = w4r[a, 0:8, :]
        gw_ref[8 * a : 8 * a + 8, 128:256] = w4r[a, 8:16, :]
    gb_ref[...] = w4r[me_a, 16:18, :]
    outgoing[2].start()
    outgoing[3].start()

    taken(mid.at[pl.ds(0, ZN - 1)], i1_send, i1_recv).wait_send()
    taken(tab.at[pl.ds(0, YH * CN - 1)], i2_send, i2_recv).wait_send()
    taken(precv.at[pl.ds(0, NB - 1)], p_send, p_recv).wait_send()
    taken(gblk.at[pl.ds(0, NB - 1)], q_send, q_recv).wait_send()
    others(w1r, NB * CN, 0).wait_send()
    others(w2r, YH, 1).wait_send()
    others(w3r, ZN, 2).wait_send()
    others(w4r, NB * CN, 3).wait_send()
    for copy in outgoing:
        copy.wait()


def write_kernel(act, gfeat, gw, gb, act_out, gfeat_out, gw_out, gb_out, act_v, gfeat_v, gw_v, gb_v, sem):
    through = ((gw, gw_v, gw_out), (act, act_v, act_out), (gfeat, gfeat_v, gfeat_out), (gb, gb_v, gb_out))
    reads = [pltpu.make_async_copy(src, mid, sem.at[i]) for i, (src, mid, dst) in enumerate(through)]
    writes = [pltpu.make_async_copy(mid, dst, sem.at[4 + i]) for i, (src, mid, dst) in enumerate(through)]
    for copy in reads:
        copy.start()
    for read, write in zip(reads, writes):
        read.wait()
        write.start()
    for copy in writes:
        copy.wait()


def per_device(features, weight, out_bias, degree, edge_dst, edge_src, hub_rows, hub_count, hub_target, cotangent):
    nd = YH * ZN * CN
    hbm = pl.BlockSpec(memory_space=pltpu.HBM)
    dma = pltpu.SemaphoreType.DMA
    shapes = (
        jax.ShapeDtypeStruct((ROWS, HID), BF16),
        jax.ShapeDtypeStruct((ROWS, FIN), BF16),
        jax.ShapeDtypeStruct((FIN, HID), F32),
        jax.ShapeDtypeStruct((2, 128), F32),
    )
    results = pl.pallas_call(
        kernel,
        out_shape=shapes,
        in_specs=[hbm] * 10,
        out_specs=(hbm,) * 4,
        scratch_shapes=[
            pltpu.VMEM((ROWS, FIN), BF16),
            pltpu.VMEM((FIN, HID), BF16),
            pltpu.VMEM((1, HID), F32),
            pltpu.VMEM((1, ROWS), jnp.int32),
            pltpu.VMEM((NB, 1, EB), jnp.int32),
            pltpu.VMEM((NB, 1, EB), jnp.int32),
            pltpu.VMEM((HUB, HUB), jnp.int32),
            pltpu.VMEM((1, HUB), jnp.int32),
            pltpu.VMEM((HUB, HUB), jnp.int32),
            pltpu.VMEM((ROWS, HID), BF16),
            pltpu.VMEM((ROWS, HID), BF16),
            pltpu.VMEM((ROWS, FIN), BF16),
            pltpu.VMEM((FIN, HID), F32),
            pltpu.VMEM((2, 128), F32),
            pltpu.VMEM((nd, ROWS, FIN), BF16),
            pltpu.VMEM((nd, ROWS, FIN), BF16),
            pltpu.VMEM((ROWS, FIN), F32),
            pltpu.VMEM((ROWS, FIN), F32),
            pltpu.VMEM((NB, ROWS, ROWS), BF16),
            pltpu.VMEM((NB, ROWS, FIN), BF16),
            pltpu.VMEM((NB, ROWS, FIN), BF16),
            pltpu.VMEM((NB, ROWS, FIN), BF16),
            pltpu.VMEM((ZN, YH * CN, 1, 2 * HUB), jnp.int32),
            pltpu.VMEM((nd, 2 * HUB), jnp.int32),
            pltpu.VMEM((ZN, YH * CN, 1, 2 * HUB), jnp.int32),
            pltpu.VMEM((ZN, YH * CN, 1, 2 * HUB), jnp.int32),
            pltpu.VMEM((NB * CN, 18, 128), F32),
            pltpu.VMEM((NB * CN, 18, 128), F32),
            pltpu.VMEM((YH, 18, 128), F32),
            pltpu.VMEM((ZN, 18, 128), F32),
            pltpu.VMEM((NB * CN, 18, 128), F32),
            dma((10,)), dma((4,)), dma(()), dma((nd,)), dma(()), dma((nd,)),
            dma(()), dma(()), dma(()), dma(()), dma(()), dma(()), dma(()), dma(()), dma((4,)), dma((4,)),
        ],
        compiler_params=pltpu.CompilerParams(
            collective_id=0, has_side_effects=True, vmem_limit_bytes=60 * 1024 * 1024
        ),
    )(
        features, weight, out_bias.reshape(1, HID), degree.reshape(1, ROWS), edge_dst, edge_src,
        hub_rows, hub_count, hub_target, cotangent,
    )
    act, gfeat, gw, gb = pl.pallas_call(
        write_kernel,
        out_shape=shapes,
        in_specs=[hbm] * 4,
        out_specs=(hbm,) * 4,
        scratch_shapes=[pltpu.VMEM(shape.shape, shape.dtype) for shape in shapes] + [dma((8,))],
        compiler_params=pltpu.CompilerParams(vmem_limit_bytes=60 * 1024 * 1024),
    )(*results)
    return act, gfeat, gw, gb.reshape(HID)


def solution(mesh):
    return jax.shard_map(
        per_device,
        mesh=mesh,
        in_specs=(
            P(("dom", "blk"), None),
            P(),
            P(),
            P(("dom", "blk")),
            P("dom", "blk", None),
            P("dom", "blk", None),
            P("dom", "blk", None, None),
            P("dom", "blk", None),
            P("dom", "blk", None, None),
            P(("dom", "blk"), None),
        ),
        out_specs=(P(("dom", "blk"), None), P(("dom", "blk"), None), P(), P()),
        check_vma=False,
    )
```

time: 87.8 us -> 73.1 us (0.83)
  local copies, waits for them, and re-layouts: 8.5 us -> 0 us
  Pallas kernels: 78.1 us -> 72.3 us
    unnamed x24 -> x0, local copies, waits for them, and re-layouts: 8.5 us -> none
    pallas_call x1 -> x2, Pallas kernels: 78.1 us -> 72.3 us  [the longest x1 70.7 us: per_device(): pl.pallas_call(kernel, out_shape=shapes, in_specs=[hbm] * 10, out_specs=(...]
where the time goes in v2:
time: 73.1 us; the launch traced here: 73 us
  Pallas kernels  72.3 us (99%)
    pallas_call x1, Pallas kernels, per_device(): pl.pallas_call(kernel, out_shape=shapes, in_specs=[hbm] * 10, out_specs=(...  70.7 us
    pallas_call x1, Pallas kernels, per_device(): pl.pallas_call(write_kernel, out_shape=shapes, in_specs=[hbm] * 4, out_sp...  1.66 us

profile of v2, /device:TPU:1, one launch (start us, length us, event | category | flops | bytes accessed | tf_op | source)
XLA Modules:
  0.0 73.0 jit_solution(1289342019902484544)
XLA Ops:
  0.6 70.7 %shard_map.129 = (bf16[128,256]{1,0:T(8,128)(2,1)}, bf16[128,128]{1,0:T(8,128)(2,1)}, f32[128,256]{1,0:T(8,128)}, f32[2,128]{1,0:T(2,128)}) custom-call(bf16[128,128]{1,0:T(8,128)(2,1)} %feat_hbm.1, bf16[128,256]{1,0:T(8,128)(2,1)} %weight_hbm.1, f32[1,256]{1,0:T(1,128)} %bitcast.3, s32[1,128]{1,0:T(1,128)} %bitcast.4, s32[8,1,384]{2,1,0:T(1,128)} %dst_hbm.1, ...), custom_call_target="tpu_custom_call" | custom-call | tf_op jit(solution)/shard_map/pallas_call | solution.py:421
  71.3 1.7 %shard_map.130 = (bf16[128,256]{1,0:T(8,128)(2,1)}, bf16[128,128]{1,0:T(8,128)(2,1)}, f32[128,256]{1,0:T(8,128)}, f32[2,128]{1,0:T(2,128)}) custom-call(bf16[128,256]{1,0:T(8,128)(2,1)} %get-tuple-element.12.act, bf16[128,128]{1,0:T(8,128)(2,1)} %get-tuple-element.13.gfeat, f32[128,256]{1,0:T(8,128)} %get-tuple-element.14.gw, f32[2,128]{1,0:T(2,128)} %get-tuple-element.15.gb), custom_call_target="tpu_custom_call" | custom-call | tf_op jit(solution)/shard_map/pallas_call | solution.py:468

commit v3 on v2

v3 whole, which is shorter than its diff:
```python
import functools

import jax
import jax.numpy as jnp
from jax import lax
from jax.experimental import pallas as pl
from jax.experimental.pallas import tpu as pltpu
from jax.sharding import PartitionSpec as P

F32 = jnp.float32
BF16 = jnp.bfloat16
NT = (((1,), (1,)), ((), ()))
YH, ZN, CN, NB = 4, 8, 2, 8
ROWS, FIN, HID, HUB, EB = 128, 128, 256, 64, 384


def iota(shape, dim):
    return lax.broadcasted_iota(jnp.int32, shape, dim)


def mod(value, size):
    return lax.rem(value + size, size)


def column(row):
    n = row.shape[1]
    wide = jnp.broadcast_to(row.astype(F32), (n, n))
    return jnp.sum(jnp.where(iota((n, n), 0) == iota((n, n), 1), wide, 0.0), axis=1, keepdims=True)


def hot(row, size):
    return (iota((size, row.shape[1]), 0) == row).astype(F32).astype(BF16)


def kernel(
    feat_hbm, weight_hbm, bias_hbm, degree_hbm, dst_hbm, src_hbm, rows_hbm, count_hbm, target_hbm, cot_hbm,
    act_hbm, gfeat_hbm, gw_hbm, gb_hbm,
    feat_ref, weight_ref, bias_ref, degree_ref, dst_ref, src_ref, rows_ref, count_ref, target_ref, cot_ref,
    act_ref, gfeat_ref, gw_ref, gb_ref,
    xrow, grow, hacc, hout, hin, bout, bin_, own_part, counts_t, psend, precv, gblk, sendtab, loctab, mid, ya, mf, mb,
    w1s, w1r, w2r, w3r, w4r,
    in_sem, out_sem, xs_send, xs_recv, gs_send, gs_recv, h_send, h_recv, p_send, p_recv, q_send, q_recv,
    i_send, i_recv, w_send, w_recv,
):
    dom = lax.axis_index("dom")
    blk = lax.axis_index("blk")
    c = lax.rem(dom, CN)
    z = lax.rem(lax.div(dom, CN), ZN)
    y = lax.div(dom, CN * ZN)

    def at(yy, zz, cc):
        return (yy * ZN + zz) * CN + cc

    def each(count, body):
        def run(i, carry):
            body(i)
            return carry

        lax.fori_loop(1, count, run, 0)

    barrier = pltpu.get_barrier_semaphore()

    def greet(to_dom, to_blk):
        pl.semaphore_signal(barrier, inc=1, device_id=(to_dom, to_blk), device_id_type=pl.DeviceIdType.MESH)

    def greet_a(i):
        a = mod(blk * CN + c + i, NB * CN)
        greet(at(y, z, lax.rem(a, CN)), lax.div(a, CN))

    for i in range(1, ZN):
        greet(at(y, mod(z + i, ZN), c), blk)
    for i in range(1, YH):
        greet(at(mod(y + i, YH), z, c), blk)
    each(NB * CN, greet_a)

    incoming = [
        pltpu.make_async_copy(src, dst, in_sem.at[i])
        for i, (src, dst) in enumerate(
            (
                (degree_hbm, degree_ref), (feat_hbm, feat_ref), (count_hbm.at[0], count_ref),
                (rows_hbm.at[0, 0], rows_ref), (target_hbm.at[0, 0], target_ref), (dst_hbm, dst_ref),
                (src_hbm, src_ref), (weight_hbm, weight_ref), (bias_hbm, bias_ref), (cot_hbm, cot_ref),
            )
        )
    ]
    for copy in incoming:
        copy.start()

    outgoing = [
        pltpu.make_async_copy(src, dst, out_sem.at[i])
        for i, (src, dst) in enumerate(
            ((act_ref, act_hbm), (gfeat_ref, gfeat_hbm), (gw_ref, gw_hbm), (gb_ref, gb_hbm))
        )
    ]

    def remote(src, dst, send, recv, to_dom, to_blk):
        return pltpu.make_async_remote_copy(
            src_ref=src, dst_ref=dst, send_sem=send, recv_sem=recv,
            device_id=(to_dom, to_blk), device_id_type=pl.DeviceIdType.MESH,
        )

    def taken(ref, send, recv):
        return remote(ref, ref, send, recv, dom, blk)

    incoming[0].wait()
    incoming[1].wait()
    scale = lax.rsqrt(column(degree_ref[...]))
    xrow[z, c] = (scale * feat_ref[...].astype(F32)).astype(BF16)

    for i in (2, 3, 4):
        incoming[i].wait()
    live = iota((HUB, HUB), 1).astype(F32) < column(count_ref[...])
    rows = jnp.where(live, rows_ref[...], ROWS)
    target = target_ref[...]
    joint_tab = jnp.concatenate([rows, target], axis=1)
    loctab[...] = jnp.concatenate([target, rows], axis=1).reshape(YH, ZN * CN, 2 * HUB)
    for e in range(YH * ZN * CN):
        sendtab[(e // CN) % ZN, (e // (CN * ZN)) * CN + e % CN] = joint_tab[e : e + 1, :]

    def table_z(i):
        zz = mod(z + i, ZN)
        return remote(sendtab.at[zz], mid.at[c, z], i_send.at[0], i_recv.at[0], at(y, zz, c), blk)

    def table_y(i):
        yy = mod(y + i, YH)
        return remote(loctab.at[yy], ya.at[y], i_send.at[1], i_recv.at[1], at(yy, z, c), blk)

    table_relay = remote(mid.at[c], mid.at[c], i_send.at[2], i_recv.at[2], at(y, z, 1 - c), blk)

    def block_copy(buf, send, recv, zz, cc, to_dom, kind=0):
        return remote(buf.at[zz, cc], buf.at[zz, cc], send.at[kind], recv.at[zz, cc], to_dom, blk)

    def distance(j):
        half = lax.div(j + 1, 2)
        return jnp.where(lax.rem(j, 2) == 1, half, ZN - half)

    def line_sends(buf, send, recv):
        for i in (4, 3, 5, 2, 6, 1, 7):
            block_copy(buf, send, recv, z, c, at(y, mod(z + i, ZN), c)).start()
        block_copy(buf, send, recv, z, c, at(y, z, 1 - c), 1).start()

    def build(counts, zz, forward):
        keep = (iota((1, 2 * HUB), 1) < HUB) == forward
        for yy in range(YH):
            for cc in range(CN):
                mine = jnp.where(keep, ya[yy, pl.ds(zz * CN + cc, 1), :], -1)
                theirs = mid[cc, zz, yy * CN + c]
                counts[zz, yy, :, cc * ROWS : (cc + 1) * ROWS] = lax.dot_general(
                    hot(mine, ROWS), hot(theirs, ROWS), NT, preferred_element_type=F32
                ).astype(BF16)

    def line_loop(buf, send, recv, counts, prepare):
        hacc[...] = jnp.zeros_like(hacc)

        def step(j, carry):
            zz = mod(z + distance(j), ZN)
            prepare(j, zz)

            @pl.when(j < ZN - 1)
            def _():
                after = mod(z + distance(j + 1), ZN)
                block_copy(buf, send, recv, after, c, dom).wait_recv()
                block_copy(buf, send, recv, after, c, at(y, z, 1 - c), 1).start()

            block_copy(buf, send, recv, zz, 1 - c, dom).wait_recv()
            part = jnp.dot(
                counts[zz].reshape(YH * ROWS, CN * ROWS), buf[zz].reshape(CN * ROWS, FIN), preferred_element_type=F32
            )
            hacc[...] += part.reshape(YH, ROWS, FIN)
            return carry

        lax.fori_loop(0, ZN, step, 0)

    def sum_sends(out, inn, which):
        for i in (2, 1, 3):
            yy = mod(y + i, YH)
            out[yy] = hacc[yy].astype(BF16)
            remote(out.at[yy], inn.at[y], h_send.at[which], h_recv.at[which], at(yy, z, c), blk).start()
        inn[y] = jnp.zeros((ROWS, FIN), BF16)

    def sums(inn, which):
        return taken(inn.at[pl.ds(0, YH - 1)], h_send.at[which], h_recv.at[which])

    pl.semaphore_wait(barrier, (NB * CN - 1) + (ZN - 1) + (YH - 1))

    for i in (4, 3, 5, 2, 6, 1, 7):
        table_z(i).start()
    line_sends(xrow, xs_send, xs_recv)
    for i in (2, 1, 3):
        table_y(i).start()
    mid[c, z] = sendtab[z]
    ya[y] = loctab[y]

    incoming[5].wait()
    incoming[6].wait()

    def part_copy(a):
        return remote(psend.at[a], precv.at[blk], p_send, p_recv, dom, a)

    def local_part(i, carry):
        a = mod(blk + 1 + i, NB)
        dst_hot = hot(dst_ref[a], ROWS)
        src_hot = hot(src_ref[a], ROWS)
        count = lax.dot_general(dst_hot, src_hot, NT, preferred_element_type=F32).astype(BF16)
        counts_t[a] = lax.dot_general(src_hot, dst_hot, NT, preferred_element_type=F32).astype(BF16)
        part = jnp.dot(count, xrow[z, c], preferred_element_type=F32)

        @pl.when(i < NB - 1)
        def _():
            psend[a] = part.astype(BF16)
            part_copy(a).start()

        @pl.when(i == NB - 1)
        def _():
            own_part[...] = part
            precv[a] = jnp.zeros((ROWS, FIN), BF16)

        return carry

    lax.fori_loop(0, NB, local_part, 0)

    taken(mid.at[c, pl.ds(0, ZN - 1)], i_send.at[0], i_recv.at[0]).wait_recv()
    table_relay.start()
    taken(ya.at[pl.ds(0, YH - 1)], i_send.at[1], i_recv.at[1]).wait_recv()
    remote(mid.at[1 - c], mid.at[1 - c], i_send.at[2], i_recv.at[2], dom, blk).wait_recv()

    line_loop(xrow, xs_send, xs_recv, mf, lambda j, zz: build(mf, zz, True))
    sum_sends(hout, hin, 0)

    def build_back(zz, carry):
        build(mb, zz, False)
        return carry

    lax.fori_loop(0, ZN, build_back, 0)
    total = hacc[y] + own_part[...]
    taken(precv.at[pl.ds(0, NB - 1)], p_send, p_recv).wait_recv()
    for i in range(NB):
        total = total + precv[i].astype(F32)
    sums(hin, 0).wait_recv()
    for i in range(YH):
        total = total + hin[i].astype(F32)

    for i in (7, 8, 9):
        incoming[i].wait()
    weight = weight_ref[...]
    pre = scale * jnp.dot(total.astype(BF16), weight, preferred_element_type=F32) + bias_ref[...]
    sig = jax.nn.sigmoid(pre)
    grad_pre = cot_ref[...].astype(F32) * sig * (1.0 + pre * (1.0 - sig))
    back = (scale * grad_pre).astype(BF16)
    grad = lax.dot_general(back, weight, NT, preferred_element_type=F32).astype(BF16)
    grow[z, c] = grad
    line_sends(grow, gs_send, gs_recv)
    gblk[blk] = grad

    def member_copy(i):
        return remote(grow.at[z, c], gblk.at[blk], q_send, q_recv, dom, mod(blk + i, NB))

    bias_term = jnp.sum(grad_pre, axis=0, keepdims=True)
    gw = jnp.dot(total.T.astype(BF16), back, preferred_element_type=F32)
    me_a = blk * CN + c
    for a in range(NB * CN):
        w1s[a, 0:8, :] = gw[8 * a : 8 * a + 8, 0:128]
        w1s[a, 8:16, :] = gw[8 * a : 8 * a + 8, 128:256]
        w1s[a, 16:17, :] = bias_term[:, 0:128]
        w1s[a, 17:18, :] = bias_term[:, 128:256]
    w1r[me_a] = w1s[me_a]

    def w1_copy(i):
        a = mod(me_a + i, NB * CN)
        return remote(
            w1s.at[a], w1r.at[me_a], w_send.at[0], w_recv.at[0], at(y, z, lax.rem(a, CN)), lax.div(a, CN)
        )

    def w2_copy(i):
        return remote(w2r.at[y], w2r.at[y], w_send.at[1], w_recv.at[1], at(mod(y + i, YH), z, c), blk)

    def w3_copy(i):
        return remote(w3r.at[z], w3r.at[z], w_send.at[2], w_recv.at[2], at(y, mod(z + i, ZN), c), blk)

    def w4_copy(i):
        a = mod(me_a + i, NB * CN)
        return remote(
            w4r.at[me_a], w4r.at[me_a], w_send.at[3], w_recv.at[3], at(y, z, lax.rem(a, CN)), lax.div(a, CN)
        )

    def others(ref, count, which):
        return taken(ref.at[pl.ds(0, count - 1)], w_send.at[which], w_recv.at[which])

    each(NB * CN, lambda i: w1_copy(i).start())
    each(NB, lambda i: member_copy(i).start())
    act_ref[...] = (pre * sig).astype(BF16)
    outgoing[0].start()

    def backward_extra(j, zz):
        @pl.when(j == 4)
        def _():
            others(w1r, NB * CN, 0).wait_recv()
            w2r[y] = jnp.sum(w1r[...], axis=0)
            each(YH, lambda i: w2_copy(i).start())

    line_loop(grow, gs_send, gs_recv, mb, backward_extra)
    sum_sends(bout, bin_, 1)

    taken(gblk.at[pl.ds(0, NB - 1)], q_send, q_recv).wait_recv()
    total_back = hacc[y]
    for a in range(NB):
        total_back = total_back + jnp.dot(counts_t[a], gblk[a], preferred_element_type=F32)

    others(w2r, YH, 1).wait_recv()
    w3r[z] = jnp.sum(w2r[...], axis=0)
    each(ZN, lambda i: w3_copy(i).start())

    sums(bin_, 1).wait_recv()
    for i in range(YH):
        total_back = total_back + bin_[i].astype(F32)
    gfeat_ref[...] = (scale * total_back).astype(BF16)
    outgoing[1].start()

    others(w3r, ZN, 2).wait_recv()
    w4r[me_a] = jnp.sum(w3r[...], axis=0)
    each(NB * CN, lambda i: w4_copy(i).start())

    others(w4r, NB * CN, 3).wait_recv()
    for a in range(NB * CN):
        gw_ref[8 * a : 8 * a + 8, 0:128] = w4r[a, 0:8, :]
        gw_ref[8 * a : 8 * a + 8, 128:256] = w4r[a, 8:16, :]
    gb_ref[...] = w4r[me_a, 16:18, :]
    outgoing[2].start()
    outgoing[3].start()

    for send, recv in ((xs_send, xs_recv), (gs_send, gs_recv)):
        taken(psend.at[pl.ds(0, ZN - 1)], send.at[0], recv.at[0, 0]).wait_send()
        taken(psend, send.at[1], recv.at[0, 0]).wait_send()
    taken(mid.at[c, pl.ds(0, ZN - 1)], i_send.at[0], i_recv.at[0]).wait_send()
    taken(ya.at[pl.ds(0, YH - 1)], i_send.at[1], i_recv.at[1]).wait_send()
    table_relay.wait_send()
    sums(hin, 0).wait_send()
    sums(bin_, 1).wait_send()
    taken(precv.at[pl.ds(0, NB - 1)], p_send, p_recv).wait_send()
    taken(gblk.at[pl.ds(0, NB - 1)], q_send, q_recv).wait_send()
    others(w1r, NB * CN, 0).wait_send()
    others(w2r, YH, 1).wait_send()
    others(w3r, ZN, 2).wait_send()
    others(w4r, NB * CN, 3).wait_send()
    for copy in outgoing:
        copy.wait()


def write_kernel(act, gfeat, gw, gb, act_out, gfeat_out, gw_out, gb_out, act_v, gfeat_v, gw_v, gb_v, sem):
    through = ((gw, gw_v, gw_out), (act, act_v, act_out), (gfeat, gfeat_v, gfeat_out), (gb, gb_v, gb_out))
    reads = [pltpu.make_async_copy(src, mid, sem.at[i]) for i, (src, mid, dst) in enumerate(through)]
    writes = [pltpu.make_async_copy(mid, dst, sem.at[4 + i]) for i, (src, mid, dst) in enumerate(through)]
    for copy in reads:
        copy.start()
    for read, write in zip(reads, writes):
        read.wait()
        write.start()
    for copy in writes:
        copy.wait()


def per_device(features, weight, out_bias, degree, edge_dst, edge_src, hub_rows, hub_count, hub_target, cotangent):
    hbm = pl.BlockSpec(memory_space=pltpu.HBM)
    dma = pltpu.SemaphoreType.DMA
    shapes = (
        jax.ShapeDtypeStruct((ROWS, HID), BF16),
        jax.ShapeDtypeStruct((ROWS, FIN), BF16),
        jax.ShapeDtypeStruct((FIN, HID), F32),
        jax.ShapeDtypeStruct((2, 128), F32),
    )
    results = pl.pallas_call(
        kernel,
        out_shape=shapes,
        in_specs=[hbm] * 10,
        out_specs=(hbm,) * 4,
        scratch_shapes=[
            pltpu.VMEM((ROWS, FIN), BF16),
            pltpu.VMEM((FIN, HID), BF16),
            pltpu.VMEM((1, HID), F32),
            pltpu.VMEM((1, ROWS), jnp.int32),
            pltpu.VMEM((NB, 1, EB), jnp.int32),
            pltpu.VMEM((NB, 1, EB), jnp.int32),
            pltpu.VMEM((HUB, HUB), jnp.int32),
            pltpu.VMEM((1, HUB), jnp.int32),
            pltpu.VMEM((HUB, HUB), jnp.int32),
            pltpu.VMEM((ROWS, HID), BF16),
            pltpu.VMEM((ROWS, HID), BF16),
            pltpu.VMEM((ROWS, FIN), BF16),
            pltpu.VMEM((FIN, HID), F32),
            pltpu.VMEM((2, 128), F32),
            pltpu.VMEM((ZN, CN, ROWS, FIN), BF16),
            pltpu.VMEM((ZN, CN, ROWS, FIN), BF16),
            pltpu.VMEM((YH, ROWS, FIN), F32),
            pltpu.VMEM((YH, ROWS, FIN), BF16),
            pltpu.VMEM((YH, ROWS, FIN), BF16),
            pltpu.VMEM((YH, ROWS, FIN), BF16),
            pltpu.VMEM((YH, ROWS, FIN), BF16),
            pltpu.VMEM((ROWS, FIN), F32),
            pltpu.VMEM((NB, ROWS, ROWS), BF16),
            pltpu.VMEM((NB, ROWS, FIN), BF16),
            pltpu.VMEM((NB, ROWS, FIN), BF16),
            pltpu.VMEM((NB, ROWS, FIN), BF16),
            pltpu.VMEM((ZN, YH * CN, 1, 2 * HUB), jnp.int32),
            pltpu.VMEM((YH, ZN * CN, 2 * HUB), jnp.int32),
            pltpu.VMEM((CN, ZN, YH * CN, 1, 2 * HUB), jnp.int32),
            pltpu.VMEM((YH, ZN * CN, 2 * HUB), jnp.int32),
            pltpu.VMEM((ZN, YH, ROWS, CN * ROWS), BF16),
            pltpu.VMEM((ZN, YH, ROWS, CN * ROWS), BF16),
            pltpu.VMEM((NB * CN, 18, 128), F32),
            pltpu.VMEM((NB * CN, 18, 128), F32),
            pltpu.VMEM((YH, 18, 128), F32),
            pltpu.VMEM((ZN, 18, 128), F32),
            pltpu.VMEM((NB * CN, 18, 128), F32),
            dma((10,)), dma((4,)), dma((2,)), dma((ZN, CN)), dma((2,)), dma((ZN, CN)),
            dma((2,)), dma((2,)), dma(()), dma(()), dma(()), dma(()), dma((3,)), dma((3,)), dma((4,)), dma((4,)),
        ],
        compiler_params=pltpu.CompilerParams(
            collective_id=0, has_side_effects=True, vmem_limit_bytes=60 * 1024 * 1024
        ),
    )(
        features, weight, out_bias.reshape(1, HID), degree.reshape(1, ROWS), edge_dst, edge_src,
        hub_rows, hub_count, hub_target, cotangent,
    )
    act, gfeat, gw, gb = pl.pallas_call(
        write_kernel,
        out_shape=shapes,
        in_specs=[hbm] * 4,
        out_specs=(hbm,) * 4,
        scratch_shapes=[pltpu.VMEM(shape.shape, shape.dtype) for shape in shapes] + [dma((8,))],
        compiler_params=pltpu.CompilerParams(vmem_limit_bytes=60 * 1024 * 1024),
    )(*results)
    return act, gfeat, gw, gb.reshape(HID)


def solution(mesh):
    return jax.shard_map(
        per_device,
        mesh=mesh,
        in_specs=(
            P(("dom", "blk"), None),
            P(),
            P(),
            P(("dom", "blk")),
            P("dom", "blk", None),
            P("dom", "blk", None),
            P("dom", "blk", None, None),
            P("dom", "blk", None),
            P("dom", "blk", None, None),
            P(("dom", "blk"), None),
        ),
        out_specs=(P(("dom", "blk"), None), P(("dom", "blk"), None), P(), P()),
        check_vma=False,
    )
```

time: 73.1 us -> 61.5 us (0.84)
  Pallas kernels: 72.3 us -> 60.6 us
    pallas_call x1, Pallas kernels: 70.7 us -> 59 us  [per_device(): pl.pallas_call(kernel, out_shape=shapes, in_specs=[hbm] * 10, out_specs=(...]
where the time goes in v3:
time: 61.5 us; the launch traced here: 61.3 us
  Pallas kernels  60.6 us (99%)
  between operations  0.64 us (1%)
    pallas_call x1, Pallas kernels, per_device(): pl.pallas_call(kernel, out_shape=shapes, in_specs=[hbm] * 10, out_specs=(...  59 us
    pallas_call x1, Pallas kernels, per_device(): pl.pallas_call(write_kernel, out_shape=shapes, in_specs=[hbm] * 4, out_sp...  1.66 us

profile of v3, /device:TPU:1, one launch (start us, length us, event | category | flops | bytes accessed | tf_op | source)
XLA Modules:
  0.0 61.3 jit_solution(12146080384773542757)
XLA Ops:
  0.6 59.0 %shard_map.129 = (bf16[128,256]{1,0:T(8,128)(2,1)}, bf16[128,128]{1,0:T(8,128)(2,1)}, f32[128,256]{1,0:T(8,128)}, f32[2,128]{1,0:T(2,128)}) custom-call(bf16[128,128]{1,0:T(8,128)(2,1)} %feat_hbm.1, bf16[128,256]{1,0:T(8,128)(2,1)} %weight_hbm.1, f32[1,256]{1,0:T(1,128)} %bitcast.3, s32[1,128]{1,0:T(1,128)} %bitcast.4, s32[8,1,384]{2,1,0:T(1,128)} %dst_hbm.1, ...), custom_call_target="tpu_custom_call" | custom-call | tf_op jit(solution)/shard_map/pallas_call | solution.py:371
  59.6 1.7 %shard_map.130 = (bf16[128,256]{1,0:T(8,128)(2,1)}, bf16[128,128]{1,0:T(8,128)(2,1)}, f32[128,256]{1,0:T(8,128)}, f32[2,128]{1,0:T(2,128)}) custom-call(bf16[128,256]{1,0:T(8,128)(2,1)} %get-tuple-element.12.act, bf16[128,128]{1,0:T(8,128)(2,1)} %get-tuple-element.13.gfeat, f32[128,256]{1,0:T(8,128)} %get-tuple-element.14.gw, f32[2,128]{1,0:T(2,128)} %get-tuple-element.15.gb), custom_call_target="tpu_custom_call" | custom-call | tf_op jit(solution)/shard_map/pallas_call | solution.py:424

commit v4 on v3

--- a/solution.py
+++ b/solution.py
@@ -38,7 +38,7 @@
     feat_ref, weight_ref, bias_ref, degree_ref, dst_ref, src_ref, rows_ref, count_ref, target_ref, cot_ref,
     act_ref, gfeat_ref, gw_ref, gb_ref,
     xrow, grow, hacc, hout, hin, bout, bin_, own_part, counts_t, psend, precv, gblk, sendtab, loctab, mid, ya, mf, mb,
-    w1s, w1r, w2r, w3r, w4r,
+    w1s, w1r, w2r, w3r,
     in_sem, out_sem, xs_send, xs_recv, gs_send, gs_recv, h_send, h_recv, p_send, p_recv, q_send, q_recv,
     i_send, i_recv, w_send, w_recv,
 ):
@@ -63,15 +63,13 @@
     def greet(to_dom, to_blk):
         pl.semaphore_signal(barrier, inc=1, device_id=(to_dom, to_blk), device_id_type=pl.DeviceIdType.MESH)
 
-    def greet_a(i):
-        a = mod(blk * CN + c + i, NB * CN)
-        greet(at(y, z, lax.rem(a, CN)), lax.div(a, CN))
-
     for i in range(1, ZN):
         greet(at(y, mod(z + i, ZN), c), blk)
     for i in range(1, YH):
         greet(at(mod(y + i, YH), z, c), blk)
-    each(NB * CN, greet_a)
+    greet(at(y, z, 1 - c), blk)
+    for i in range(1, NB):
+        greet(dom, mod(blk + i, NB))
 
     incoming = [
         pltpu.make_async_copy(src, dst, in_sem.at[i])
@@ -135,7 +133,7 @@
         return jnp.where(lax.rem(j, 2) == 1, half, ZN - half)
 
     def line_sends(buf, send, recv):
-        for i in (4, 3, 5, 2, 6, 1, 7):
+        for i in (1, 7, 2, 6, 3, 5, 4):
             block_copy(buf, send, recv, z, c, at(y, mod(z + i, ZN), c)).start()
         block_copy(buf, send, recv, z, c, at(y, z, 1 - c), 1).start()
 
@@ -181,7 +179,7 @@
     def sums(inn, which):
         return taken(inn.at[pl.ds(0, YH - 1)], h_send.at[which], h_recv.at[which])
 
-    pl.semaphore_wait(barrier, (NB * CN - 1) + (ZN - 1) + (YH - 1))
+    pl.semaphore_wait(barrier, (NB - 1) + (ZN - 1) + (YH - 1) + 1)
 
     for i in (4, 3, 5, 2, 6, 1, 7):
         table_z(i).start()
@@ -225,6 +223,7 @@
     remote(mid.at[1 - c], mid.at[1 - c], i_send.at[2], i_recv.at[2], dom, blk).wait_recv()
 
     line_loop(xrow, xs_send, xs_recv, mf, lambda j, zz: build(mf, zz, True))
+    taken(precv.at[pl.ds(0, NB - 1)], p_send, p_recv).wait_recv()
     sum_sends(hout, hin, 0)
 
     def build_back(zz, carry):
@@ -233,7 +232,6 @@
 
     lax.fori_loop(0, ZN, build_back, 0)
     total = hacc[y] + own_part[...]
-    taken(precv.at[pl.ds(0, NB - 1)], p_send, p_recv).wait_recv()
     for i in range(NB):
         total = total + precv[i].astype(F32)
     sums(hin, 0).wait_recv()
@@ -248,55 +246,54 @@
     grad_pre = cot_ref[...].astype(F32) * sig * (1.0 + pre * (1.0 - sig))
     back = (scale * grad_pre).astype(BF16)
     grad = lax.dot_general(back, weight, NT, preferred_element_type=F32).astype(BF16)
+    bias_term = jnp.sum(grad_pre, axis=0, keepdims=True)
+    gw = jnp.dot(total.T.astype(BF16), back, preferred_element_type=F32)
     grow[z, c] = grad
     line_sends(grow, gs_send, gs_recv)
+    me_a = blk * YH + y
+    me_b = z * CN + c
+    for a in range(NB * YH):
+        g, h = a // 2, a % 2
+        w1s[a, 0:8, :] = gw[8 * g : 8 * g + 8, 128 * h : 128 * h + 128]
+        w1s[a, 8:9, :] = bias_term[:, 0:128]
+        w1s[a, 9:10, :] = bias_term[:, 128:256]
+    w1r[me_a] = w1s[me_a]
+
+    def peer(i):
+        a = mod(me_a + i, NB * YH)
+        return a, at(lax.rem(a, YH), z, c), lax.div(a, YH)
+
+    def w1_copy(i):
+        a, to_dom, to_blk = peer(i)
+        return remote(w1s.at[a], w1r.at[me_a], w_send.at[0], w_recv.at[0], to_dom, to_blk)
+
+    def w2_copy(i):
+        b = mod(me_b + i, ZN * CN)
+        return remote(w2r.at[me_b], w2r.at[me_b], w_send.at[1], w_recv.at[1], y * (ZN * CN) + b, blk)
+
+    def w3_copy(i):
+        a, to_dom, to_blk = peer(i)
+        return remote(w3r.at[me_a], w3r.at[me_a], w_send.at[2], w_recv.at[2], to_dom, to_blk)
+
     gblk[blk] = grad
 
     def member_copy(i):
         return remote(grow.at[z, c], gblk.at[blk], q_send, q_recv, dom, mod(blk + i, NB))
 
-    bias_term = jnp.sum(grad_pre, axis=0, keepdims=True)
-    gw = jnp.dot(total.T.astype(BF16), back, preferred_element_type=F32)
-    me_a = blk * CN + c
-    for a in range(NB * CN):
-        w1s[a, 0:8, :] = gw[8 * a : 8 * a + 8, 0:128]
-        w1s[a, 8:16, :] = gw[8 * a : 8 * a + 8, 128:256]
-        w1s[a, 16:17, :] = bias_term[:, 0:128]
-        w1s[a, 17:18, :] = bias_term[:, 128:256]
-    w1r[me_a] = w1s[me_a]
-
-    def w1_copy(i):
-        a = mod(me_a + i, NB * CN)
-        return remote(
-            w1s.at[a], w1r.at[me_a], w_send.at[0], w_recv.at[0], at(y, z, lax.rem(a, CN)), lax.div(a, CN)
-        )
-
-    def w2_copy(i):
-        return remote(w2r.at[y], w2r.at[y], w_send.at[1], w_recv.at[1], at(mod(y + i, YH), z, c), blk)
-
-    def w3_copy(i):
-        return remote(w3r.at[z], w3r.at[z], w_send.at[2], w_recv.at[2], at(y, mod(z + i, ZN), c), blk)
-
-    def w4_copy(i):
-        a = mod(me_a + i, NB * CN)
-        return remote(
-            w4r.at[me_a], w4r.at[me_a], w_send.at[3], w_recv.at[3], at(y, z, lax.rem(a, CN)), lax.div(a, CN)
-        )
-
     def others(ref, count, which):
         return taken(ref.at[pl.ds(0, count - 1)], w_send.at[which], w_recv.at[which])
 
-    each(NB * CN, lambda i: w1_copy(i).start())
+    each(NB * YH, lambda i: w1_copy(i).start())
     each(NB, lambda i: member_copy(i).start())
     act_ref[...] = (pre * sig).astype(BF16)
     outgoing[0].start()
 
     def backward_extra(j, zz):
-        @pl.when(j == 4)
+        @pl.when(j == 6)
         def _():
-            others(w1r, NB * CN, 0).wait_recv()
-            w2r[y] = jnp.sum(w1r[...], axis=0)
-            each(YH, lambda i: w2_copy(i).start())
+            others(w1r, NB * YH, 0).wait_recv()
+            w2r[me_b] = jnp.sum(w1r[...], axis=0)
+            each(ZN * CN, lambda i: w2_copy(i).start())
 
     line_loop(grow, gs_send, gs_recv, mb, backward_extra)
     sum_sends(bout, bin_, 1)
@@ -306,9 +303,9 @@
     for a in range(NB):
         total_back = total_back + jnp.dot(counts_t[a], gblk[a], preferred_element_type=F32)
 
-    others(w2r, YH, 1).wait_recv()
-    w3r[z] = jnp.sum(w2r[...], axis=0)
-    each(ZN, lambda i: w3_copy(i).start())
+    others(w2r, ZN * CN, 1).wait_recv()
+    w3r[me_a] = jnp.sum(w2r[...], axis=0)
+    each(NB * YH, lambda i: w3_copy(i).start())
 
     sums(bin_, 1).wait_recv()
     for i in range(YH):
@@ -316,15 +313,11 @@
     gfeat_ref[...] = (scale * total_back).astype(BF16)
     outgoing[1].start()
 
-    others(w3r, ZN, 2).wait_recv()
-    w4r[me_a] = jnp.sum(w3r[...], axis=0)
-    each(NB * CN, lambda i: w4_copy(i).start())
-
-    others(w4r, NB * CN, 3).wait_recv()
-    for a in range(NB * CN):
-        gw_ref[8 * a : 8 * a + 8, 0:128] = w4r[a, 0:8, :]
-        gw_ref[8 * a : 8 * a + 8, 128:256] = w4r[a, 8:16, :]
-    gb_ref[...] = w4r[me_a, 16:18, :]
+    others(w3r, NB * YH, 2).wait_recv()
+    for a in range(NB * YH):
+        g, h = a // 2, a % 2
+        gw_ref[8 * g : 8 * g + 8, 128 * h : 128 * h + 128] = w3r[a, 0:8, :]
+    gb_ref[...] = w3r[me_a, 8:10, :]
     outgoing[2].start()
     outgoing[3].start()
 
@@ -338,10 +331,9 @@
     sums(bin_, 1).wait_send()
     taken(precv.at[pl.ds(0, NB - 1)], p_send, p_recv).wait_send()
     taken(gblk.at[pl.ds(0, NB - 1)], q_send, q_recv).wait_send()
-    others(w1r, NB * CN, 0).wait_send()
-    others(w2r, YH, 1).wait_send()
-    others(w3r, ZN, 2).wait_send()
-    others(w4r, NB * CN, 3).wait_send()
+    others(w1r, NB * YH, 0).wait_send()
+    others(w2r, ZN * CN, 1).wait_send()
+    others(w3r, NB * YH, 2).wait_send()
     for copy in outgoing:
         copy.wait()
 
@@ -406,13 +398,12 @@
             pltpu.VMEM((YH, ZN * CN, 2 * HUB), jnp.int32),
             pltpu.VMEM((ZN, YH, ROWS, CN * ROWS), BF16),
             pltpu.VMEM((ZN, YH, ROWS, CN * ROWS), BF16),
-            pltpu.VMEM((NB * CN, 18, 128), F32),
-            pltpu.VMEM((NB * CN, 18, 128), F32),
-            pltpu.VMEM((YH, 18, 128), F32),
-            pltpu.VMEM((ZN, 18, 128), F32),
-            pltpu.VMEM((NB * CN, 18, 128), F32),
+            pltpu.VMEM((NB * YH, 10, 128), F32),
+            pltpu.VMEM((NB * YH, 10, 128), F32),
+            pltpu.VMEM((ZN * CN, 10, 128), F32),
+            pltpu.VMEM((NB * YH, 10, 128), F32),
             dma((10,)), dma((4,)), dma((2,)), dma((ZN, CN)), dma((2,)), dma((ZN, CN)),
-            dma((2,)), dma((2,)), dma(()), dma(()), dma(()), dma(()), dma((3,)), dma((3,)), dma((4,)), dma((4,)),
+            dma((2,)), dma((2,)), dma(()), dma(()), dma(()), dma(()), dma((3,)), dma((3,)), dma((3,)), dma((3,)),
         ],
         compiler_params=pltpu.CompilerParams(
             collective_id=0, has_side_effects=True, vmem_limit_bytes=60 * 1024 * 1024

time: 61.5 us -> 59.1 us (0.961)
  Pallas kernels: 60.6 us -> 58.3 us
    pallas_call x1, Pallas kernels: 59 us -> 56.7 us  [per_device(): pl.pallas_call(kernel, out_shape=shapes, in_specs=[hbm] * 10, out_specs=(...]
where the time goes in v4:
time: 59.1 us; the launch traced here: 59 us
  Pallas kernels  58.3 us (99%)
  between operations  0.64 us (1%)
    pallas_call x1, Pallas kernels, per_device(): pl.pallas_call(kernel, out_shape=shapes, in_specs=[hbm] * 10, out_specs=(...  56.7 us
    pallas_call x1, Pallas kernels, per_device(): pl.pallas_call(write_kernel, out_shape=shapes, in_specs=[hbm] * 4, out_sp...  1.66 us

profile of v4, /device:TPU:1, one launch (start us, length us, event | category | flops | bytes accessed | tf_op | source)
XLA Modules:
  0.0 59.0 jit_solution(2103765972154066590)
XLA Ops:
  0.6 56.7 %shard_map.129 = (bf16[128,256]{1,0:T(8,128)(2,1)}, bf16[128,128]{1,0:T(8,128)(2,1)}, f32[128,256]{1,0:T(8,128)}, f32[2,128]{1,0:T(2,128)}) custom-call(bf16[128,128]{1,0:T(8,128)(2,1)} %feat_hbm.1, bf16[128,256]{1,0:T(8,128)(2,1)} %weight_hbm.1, f32[1,256]{1,0:T(1,128)} %bitcast.3, s32[1,128]{1,0:T(1,128)} %bitcast.4, s32[8,1,384]{2,1,0:T(1,128)} %dst_hbm.1, ...), custom_call_target="tpu_custom_call" | custom-call | tf_op jit(solution)/shard_map/pallas_call | solution.py:363
  57.3 1.7 %shard_map.130 = (bf16[128,256]{1,0:T(8,128)(2,1)}, bf16[128,128]{1,0:T(8,128)(2,1)}, f32[128,256]{1,0:T(8,128)}, f32[2,128]{1,0:T(2,128)}) custom-call(bf16[128,256]{1,0:T(8,128)(2,1)} %get-tuple-element.12.act, bf16[128,128]{1,0:T(8,128)(2,1)} %get-tuple-element.13.gfeat, f32[128,256]{1,0:T(8,128)} %get-tuple-element.14.gw, f32[2,128]{1,0:T(2,128)} %get-tuple-element.15.gb), custom_call_target="tpu_custom_call" | custom-call | tf_op jit(solution)/shard_map/pallas_call | solution.py:415

commit v5 on v4

--- a/solution.py
+++ b/solution.py
@@ -14,6 +14,17 @@
 ROWS, FIN, HID, HUB, EB = 128, 128, 256, 64, 384
 
 
+def ring(step, size):
+    return min(step, size - step)
+
+
+FAR_AY = sorted(
+    ((dx, flip, dy) for dx in range(4) for flip in range(2) for dy in range(YH) if dx or flip or dy),
+    key=lambda step: -(ring(step[0], 4) + step[1] + 2 * ring(step[2], YH)),
+)
+FAR_ZC = sorted(((dz, flip) for dz in range(ZN) for flip in range(CN) if dz or flip), key=lambda step: -ring(step[0], ZN))
+
+
 def iota(shape, dim):
     return lax.broadcasted_iota(jnp.int32, shape, dim)
 
@@ -36,7 +47,7 @@
     feat_hbm, weight_hbm, bias_hbm, degree_hbm, dst_hbm, src_hbm, rows_hbm, count_hbm, target_hbm, cot_hbm,
     act_hbm, gfeat_hbm, gw_hbm, gb_hbm,
     feat_ref, weight_ref, bias_ref, degree_ref, dst_ref, src_ref, rows_ref, count_ref, target_ref, cot_ref,
-    act_ref, gfeat_ref, gw_ref, gb_ref,
+    act_ref, gfeat_ref, gb_ref,
     xrow, grow, hacc, hout, hin, bout, bin_, own_part, counts_t, psend, precv, gblk, sendtab, loctab, mid, ya, mf, mb,
     w1s, w1r, w2r, w3r,
     in_sem, out_sem, xs_send, xs_recv, gs_send, gs_recv, h_send, h_recv, p_send, p_recv, q_send, q_recv,
@@ -85,9 +96,9 @@
         copy.start()
 
     outgoing = [
-        pltpu.make_async_copy(src, dst, out_sem.at[i])
+        pltpu.make_async_copy(src, dst, out_sem.at[3 if i == 2 else i])
         for i, (src, dst) in enumerate(
-            ((act_ref, act_hbm), (gfeat_ref, gfeat_hbm), (gw_ref, gw_hbm), (gb_ref, gb_hbm))
+            ((act_ref, act_hbm), (gfeat_ref, gfeat_hbm), (gb_ref, gb_hbm))
         )
     ]
 
@@ -259,21 +270,27 @@
         w1s[a, 9:10, :] = bias_term[:, 128:256]
     w1r[me_a] = w1s[me_a]
 
-    def peer(i):
-        a = mod(me_a + i, NB * YH)
-        return a, at(lax.rem(a, YH), z, c), lax.div(a, YH)
+    def peer(step):
+        dx, flip, dy = step
+        to_blk = mod(lax.div(blk, 2) + dx, 4) * 2 + (1 - lax.rem(blk, 2) if flip else lax.rem(blk, 2))
+        yy = mod(y + dy, YH)
+        return to_blk * YH + yy, at(yy, z, c), to_blk
+
+    gw_piece = gw_hbm.at[pl.ds(pl.multiple_of(me_a // 2 * 8, 8), 8), pl.ds(pl.multiple_of(me_a % 2 * 128, 128), 128)]
+    own_piece = pltpu.make_async_copy(w3r.at[me_a], gw_piece, out_sem.at[2])
 
     def w1_copy(i):
         a, to_dom, to_blk = peer(i)
         return remote(w1s.at[a], w1r.at[me_a], w_send.at[0], w_recv.at[0], to_dom, to_blk)
 
     def w2_copy(i):
-        b = mod(me_b + i, ZN * CN)
-        return remote(w2r.at[me_b], w2r.at[me_b], w_send.at[1], w_recv.at[1], y * (ZN * CN) + b, blk)
+        dz, flip = i
+        to_dom = at(y, mod(z + dz, ZN), 1 - c if flip else c)
+        return remote(w2r.at[me_b], w2r.at[me_b], w_send.at[1], w_recv.at[1], to_dom, blk)
 
     def w3_copy(i):
         a, to_dom, to_blk = peer(i)
-        return remote(w3r.at[me_a], w3r.at[me_a], w_send.at[2], w_recv.at[2], to_dom, to_blk)
+        return remote(w3r.at[me_a], gw_piece, w_send.at[2], w_recv.at[2], to_dom, to_blk)
 
     gblk[blk] = grad
 
@@ -283,29 +300,36 @@
     def others(ref, count, which):
         return taken(ref.at[pl.ds(0, count - 1)], w_send.at[which], w_recv.at[which])
 
-    each(NB * YH, lambda i: w1_copy(i).start())
+    for step in FAR_AY:
+        w1_copy(step).start()
     each(NB, lambda i: member_copy(i).start())
     act_ref[...] = (pre * sig).astype(BF16)
     outgoing[0].start()
 
     def backward_extra(j, zz):
-        @pl.when(j == 6)
+        @pl.when(j == 5)
         def _():
             others(w1r, NB * YH, 0).wait_recv()
             w2r[me_b] = jnp.sum(w1r[...], axis=0)
-            each(ZN * CN, lambda i: w2_copy(i).start())
+            for step in FAR_ZC:
+                w2_copy(step).start()
 
     line_loop(grow, gs_send, gs_recv, mb, backward_extra)
     sum_sends(bout, bin_, 1)
+
+    others(w2r, ZN * CN, 1).wait_recv()
+    summed = jnp.sum(w2r[...], axis=0)
+    w3r[me_a] = summed[0:8]
+    for step in FAR_AY:
+        w3_copy(step).start()
+    own_piece.start()
+    gb_ref[...] = summed[8:10]
+    outgoing[2].start()
 
     taken(gblk.at[pl.ds(0, NB - 1)], q_send, q_recv).wait_recv()
     total_back = hacc[y]
     for a in range(NB):
         total_back = total_back + jnp.dot(counts_t[a], gblk[a], preferred_element_type=F32)
-
-    others(w2r, ZN * CN, 1).wait_recv()
-    w3r[me_a] = jnp.sum(w2r[...], axis=0)
-    each(NB * YH, lambda i: w3_copy(i).start())
 
     sums(bin_, 1).wait_recv()
     for i in range(YH):
@@ -314,13 +338,6 @@
     outgoing[1].start()
 
     others(w3r, NB * YH, 2).wait_recv()
-    for a in range(NB * YH):
-        g, h = a // 2, a % 2
-        gw_ref[8 * g : 8 * g + 8, 128 * h : 128 * h + 128] = w3r[a, 0:8, :]
-    gb_ref[...] = w3r[me_a, 8:10, :]
-    outgoing[2].start()
-    outgoing[3].start()
-
     for send, recv in ((xs_send, xs_recv), (gs_send, gs_recv)):
         taken(psend.at[pl.ds(0, ZN - 1)], send.at[0], recv.at[0, 0]).wait_send()
         taken(psend, send.at[1], recv.at[0, 0]).wait_send()
@@ -334,6 +351,7 @@
     others(w1r, NB * YH, 0).wait_send()
     others(w2r, ZN * CN, 1).wait_send()
     others(w3r, NB * YH, 2).wait_send()
+    own_piece.wait()
     for copy in outgoing:
         copy.wait()
 
@@ -378,7 +396,6 @@
             pltpu.VMEM((ROWS, HID), BF16),
             pltpu.VMEM((ROWS, HID), BF16),
             pltpu.VMEM((ROWS, FIN), BF16),
-            pltpu.VMEM((FIN, HID), F32),
             pltpu.VMEM((2, 128), F32),
             pltpu.VMEM((ZN, CN, ROWS, FIN), BF16),
             pltpu.VMEM((ZN, CN, ROWS, FIN), BF16),
@@ -401,7 +418,7 @@
             pltpu.VMEM((NB * YH, 10, 128), F32),
             pltpu.VMEM((NB * YH, 10, 128), F32),
             pltpu.VMEM((ZN * CN, 10, 128), F32),
-            pltpu.VMEM((NB * YH, 10, 128), F32),
+            pltpu.VMEM((NB * YH, 8, 128), F32),
             dma((10,)), dma((4,)), dma((2,)), dma((ZN, CN)), dma((2,)), dma((ZN, CN)),
             dma((2,)), dma((2,)), dma(()), dma(()), dma(()), dma(()), dma((3,)), dma((3,)), dma((3,)), dma((3,)),
         ],

time: 59.1 us -> 55.8 us (0.944)
  Pallas kernels: 58.3 us -> 54.9 us
    pallas_call x1, Pallas kernels: 56.7 us -> 53.3 us  [per_device(): pl.pallas_call(kernel, out_shape=shapes, in_specs=[hbm] * 10, out_specs=(...]
where the time goes in v5:
time: 55.8 us; the launch traced here: 55.6 us
  Pallas kernels  54.9 us (98%)
  between operations  0.64 us (1%)
    pallas_call x1, Pallas kernels, per_device(): pl.pallas_call(kernel, out_shape=shapes, in_specs=[hbm] * 10, out_specs=(...  53.3 us
    pallas_call x1, Pallas kernels, per_device(): pl.pallas_call(write_kernel, out_shape=shapes, in_specs=[hbm] * 4, out_sp...  1.66 us

profile of v5, /device:TPU:1, one launch (start us, length us, event | category | flops | bytes accessed | tf_op | source)
XLA Modules:
  0.0 55.6 jit_solution(14883429152790878152)
XLA Ops:
  0.6 53.3 %shard_map.129 = (bf16[128,256]{1,0:T(8,128)(2,1)}, bf16[128,128]{1,0:T(8,128)(2,1)}, f32[128,256]{1,0:T(8,128)}, f32[2,128]{1,0:T(2,128)}) custom-call(bf16[128,128]{1,0:T(8,128)(2,1)} %feat_hbm.1, bf16[128,256]{1,0:T(8,128)(2,1)} %weight_hbm.1, f32[1,256]{1,0:T(1,128)} %bitcast.3, s32[1,128]{1,0:T(1,128)} %bitcast.4, s32[8,1,384]{2,1,0:T(1,128)} %dst_hbm.1, ...), custom_call_target="tpu_custom_call" | custom-call | tf_op jit(solution)/shard_map/pallas_call | solution.py:381
  53.9 1.7 %shard_map.130 = (bf16[128,256]{1,0:T(8,128)(2,1)}, bf16[128,128]{1,0:T(8,128)(2,1)}, f32[128,256]{1,0:T(8,128)}, f32[2,128]{1,0:T(2,128)}) custom-call(bf16[128,256]{1,0:T(8,128)(2,1)} %get-tuple-element.12.act, bf16[128,128]{1,0:T(8,128)(2,1)} %get-tuple-element.13.gfeat, f32[128,256]{1,0:T(8,128)} %get-tuple-element.14.gw, f32[2,128]{1,0:T(2,128)} %get-tuple-element.15.gb), custom_call_target="tpu_custom_call" | custom-call | tf_op jit(solution)/shard_map/pallas_call | solution.py:432

commit v6 on v5

--- a/solution.py
+++ b/solution.py
@@ -18,11 +18,14 @@
     return min(step, size - step)
 
 
-FAR_AY = sorted(
-    ((dx, flip, dy) for dx in range(4) for flip in range(2) for dy in range(YH) if dx or flip or dy),
-    key=lambda step: -(ring(step[0], 4) + step[1] + 2 * ring(step[2], YH)),
+FAR_A = sorted(
+    ((dx, flip, cross) for dx in range(4) for flip in range(2) for cross in range(CN) if dx or flip or cross),
+    key=lambda step: -(ring(step[0], 4) + step[1]),
 )
-FAR_ZC = sorted(((dz, flip) for dz in range(ZN) for flip in range(CN) if dz or flip), key=lambda step: -ring(step[0], ZN))
+FAR_B = sorted(
+    ((dy, dz) for dy in range(YH) for dz in range(ZN) if dy or dz),
+    key=lambda step: -(2 * ring(step[0], YH) + ring(step[1], ZN)),
+)
 
 
 def iota(shape, dim):
@@ -49,7 +52,7 @@
     feat_ref, weight_ref, bias_ref, degree_ref, dst_ref, src_ref, rows_ref, count_ref, target_ref, cot_ref,
     act_ref, gfeat_ref, gb_ref,
     xrow, grow, hacc, hout, hin, bout, bin_, own_part, counts_t, psend, precv, gblk, sendtab, loctab, mid, ya, mf, mb,
-    w1s, w1r, w2r, w3r,
+    w1s, w1r, w2r, w2b, w3r,
     in_sem, out_sem, xs_send, xs_recv, gs_send, gs_recv, h_send, h_recv, p_send, p_recv, q_send, q_recv,
     i_send, i_recv, w_send, w_recv,
 ):
@@ -78,9 +81,9 @@
         greet(at(y, mod(z + i, ZN), c), blk)
     for i in range(1, YH):
         greet(at(mod(y + i, YH), z, c), blk)
-    greet(at(y, z, 1 - c), blk)
-    for i in range(1, NB):
-        greet(dom, mod(blk + i, NB))
+    for i in range(1, NB * CN):
+        a = mod(blk * CN + c + i, NB * CN)
+        greet(at(y, z, lax.rem(a, CN)), lax.div(a, CN))
 
     incoming = [
         pltpu.make_async_copy(src, dst, in_sem.at[i])
@@ -190,7 +193,7 @@
     def sums(inn, which):
         return taken(inn.at[pl.ds(0, YH - 1)], h_send.at[which], h_recv.at[which])
 
-    pl.semaphore_wait(barrier, (NB - 1) + (ZN - 1) + (YH - 1) + 1)
+    pl.semaphore_wait(barrier, (NB * CN - 1) + (ZN - 1) + (YH - 1))
 
     for i in (4, 3, 5, 2, 6, 1, 7):
         table_z(i).start()
@@ -261,36 +264,61 @@
     gw = jnp.dot(total.T.astype(BF16), back, preferred_element_type=F32)
     grow[z, c] = grad
     line_sends(grow, gs_send, gs_recv)
-    me_a = blk * YH + y
-    me_b = z * CN + c
-    for a in range(NB * YH):
-        g, h = a // 2, a % 2
-        w1s[a, 0:8, :] = gw[8 * g : 8 * g + 8, 128 * h : 128 * h + 128]
-        w1s[a, 8:9, :] = bias_term[:, 0:128]
-        w1s[a, 9:10, :] = bias_term[:, 128:256]
+    me_a = blk * CN + c
+    me_b = y * ZN + z
+    for a in range(16):
+        w1s[a, 0:8, :] = gw[8 * a : 8 * a + 8, 0:128]
+        w1s[a, 8:16, :] = gw[8 * a : 8 * a + 8, 128:256]
+        w1s[a, 16:17, :] = bias_term[:, 0:128]
+        w1s[a, 17:18, :] = bias_term[:, 128:256]
     w1r[me_a] = w1s[me_a]
 
-    def peer(step):
-        dx, flip, dy = step
+    def peer_a(step):
+        dx, flip, cross = step
         to_blk = mod(lax.div(blk, 2) + dx, 4) * 2 + (1 - lax.rem(blk, 2) if flip else lax.rem(blk, 2))
-        yy = mod(y + dy, YH)
-        return to_blk * YH + yy, at(yy, z, c), to_blk
-
-    gw_piece = gw_hbm.at[pl.ds(pl.multiple_of(me_a // 2 * 8, 8), 8), pl.ds(pl.multiple_of(me_a % 2 * 128, 128), 128)]
+        to_c = 1 - c if cross else c
+        return to_blk * CN + to_c, at(y, z, to_c), to_blk
+
+    def peer_b(step):
+        dy, dz = step
+        return at(mod(y + dy, YH), mod(z + dz, ZN), c), blk
+
+    gw_piece = gw_hbm.at[pl.ds(pl.multiple_of(me_a * 8, 8), 8)]
     own_piece = pltpu.make_async_copy(w3r.at[me_a], gw_piece, out_sem.at[2])
 
     def w1_copy(i):
-        a, to_dom, to_blk = peer(i)
+        a, to_dom, to_blk = peer_a(i)
         return remote(w1s.at[a], w1r.at[me_a], w_send.at[0], w_recv.at[0], to_dom, to_blk)
 
-    def w2_copy(i):
-        dz, flip = i
-        to_dom = at(y, mod(z + dz, ZN), 1 - c if flip else c)
-        return remote(w2r.at[me_b], w2r.at[me_b], w_send.at[1], w_recv.at[1], to_dom, blk)
+    def w2_copies(i):
+        return [
+            remote(ref.at[me_b], ref.at[me_b], w_send.at[k], w_recv.at[k], *peer_b(i)) for ref, k in ((w2r, 1), (w2b, 3))
+        ]
 
     def w3_copy(i):
-        a, to_dom, to_blk = peer(i)
+        _, to_dom, to_blk = peer_a(i)
         return remote(w3r.at[me_a], gw_piece, w_send.at[2], w_recv.at[2], to_dom, to_blk)
+
+    def second():
+        others(w1r, 16, 0).wait_recv()
+        summed = jnp.sum(w1r[...], axis=0)
+        w2r[me_b] = summed[0:16].astype(BF16)
+        w2b[me_b] = summed[16:18]
+        for step in FAR_B:
+            w2_copies(step)[0].start()
+        for step in FAR_B:
+            w2_copies(step)[1].start()
+
+    def third():
+        others(w2r, 32, 1).wait_recv()
+        summed = jnp.sum(w2r[...].astype(F32), axis=0)
+        w3r[me_a] = jnp.concatenate([summed[0:8], summed[8:16]], axis=1)
+        for step in FAR_A:
+            w3_copy(step).start()
+        own_piece.start()
+        others(w2b, 32, 3).wait_recv()
+        gb_ref[...] = jnp.sum(w2b[...], axis=0)
+        outgoing[2].start()
 
     gblk[blk] = grad
 
@@ -300,32 +328,21 @@
     def others(ref, count, which):
         return taken(ref.at[pl.ds(0, count - 1)], w_send.at[which], w_recv.at[which])
 
-    for step in FAR_AY:
+    for step in FAR_A:
         w1_copy(step).start()
     each(NB, lambda i: member_copy(i).start())
     act_ref[...] = (pre * sig).astype(BF16)
     outgoing[0].start()
 
     def backward_extra(j, zz):
-        @pl.when(j == 5)
+        @pl.when(j == 2)
         def _():
-            others(w1r, NB * YH, 0).wait_recv()
-            w2r[me_b] = jnp.sum(w1r[...], axis=0)
-            for step in FAR_ZC:
-                w2_copy(step).start()
+            second()
 
     line_loop(grow, gs_send, gs_recv, mb, backward_extra)
     sum_sends(bout, bin_, 1)
 
-    others(w2r, ZN * CN, 1).wait_recv()
-    summed = jnp.sum(w2r[...], axis=0)
-    w3r[me_a] = summed[0:8]
-    for step in FAR_AY:
-        w3_copy(step).start()
-    own_piece.start()
-    gb_ref[...] = summed[8:10]
-    outgoing[2].start()
-
+    third()
     taken(gblk.at[pl.ds(0, NB - 1)], q_send, q_recv).wait_recv()
     total_back = hacc[y]
     for a in range(NB):
@@ -337,7 +354,7 @@
     gfeat_ref[...] = (scale * total_back).astype(BF16)
     outgoing[1].start()
 
-    others(w3r, NB * YH, 2).wait_recv()
+    others(w3r, 16, 2).wait_recv()
     for send, recv in ((xs_send, xs_recv), (gs_send, gs_recv)):
         taken(psend.at[pl.ds(0, ZN - 1)], send.at[0], recv.at[0, 0]).wait_send()
         taken(psend, send.at[1], recv.at[0, 0]).wait_send()
@@ -348,9 +365,10 @@
     sums(bin_, 1).wait_send()
     taken(precv.at[pl.ds(0, NB - 1)], p_send, p_recv).wait_send()
     taken(gblk.at[pl.ds(0, NB - 1)], q_send, q_recv).wait_send()
-    others(w1r, NB * YH, 0).wait_send()
-    others(w2r, ZN * CN, 1).wait_send()
-    others(w3r, NB * YH, 2).wait_send()
+    others(w1r, 16, 0).wait_send()
+    others(w2r, 32, 1).wait_send()
+    others(w2b, 32, 3).wait_send()
+    others(w3r, 16, 2).wait_send()
     own_piece.wait()
     for copy in outgoing:
         copy.wait()
@@ -415,12 +433,13 @@
             pltpu.VMEM((YH, ZN * CN, 2 * HUB), jnp.int32),
             pltpu.VMEM((ZN, YH, ROWS, CN * ROWS), BF16),
             pltpu.VMEM((ZN, YH, ROWS, CN * ROWS), BF16),
-            pltpu.VMEM((NB * YH, 10, 128), F32),
-            pltpu.VMEM((NB * YH, 10, 128), F32),
-            pltpu.VMEM((ZN * CN, 10, 128), F32),
-            pltpu.VMEM((NB * YH, 8, 128), F32),
+            pltpu.VMEM((16, 18, 128), F32),
+            pltpu.VMEM((16, 18, 128), F32),
+            pltpu.VMEM((32, 16, 128), BF16),
+            pltpu.VMEM((32, 2, 128), F32),
+            pltpu.VMEM((16, 8, HID), F32),
             dma((10,)), dma((4,)), dma((2,)), dma((ZN, CN)), dma((2,)), dma((ZN, CN)),
-            dma((2,)), dma((2,)), dma(()), dma(()), dma(()), dma(()), dma((3,)), dma((3,)), dma((3,)), dma((3,)),
+            dma((2,)), dma((2,)), dma(()), dma(()), dma(()), dma(()), dma((3,)), dma((3,)), dma((4,)), dma((4,)),
         ],
         compiler_params=pltpu.CompilerParams(
             collective_id=0, has_side_effects=True, vmem_limit_bytes=60 * 1024 * 1024

time: 55.8 us -> 54.1 us (0.970)
  Pallas kernels: 54.9 us -> 53.3 us
    pallas_call x1, Pallas kernels: 53.3 us -> 51.6 us  [per_device(): pl.pallas_call(kernel, out_shape=shapes, in_specs=[hbm] * 10, out_specs=(...]
where the time goes in v6:
time: 54.1 us; the launch traced here: 53.9 us
  Pallas kernels  53.3 us (99%)
  between operations  0.64 us (1%)
    pallas_call x1, Pallas kernels, per_device(): pl.pallas_call(kernel, out_shape=shapes, in_specs=[hbm] * 10, out_specs=(...  51.6 us
    pallas_call x1, Pallas kernels, per_device(): pl.pallas_call(write_kernel, out_shape=shapes, in_specs=[hbm] * 4, out_sp...  1.66 us

profile of v6, /device:TPU:1, one launch (start us, length us, event | category | flops | bytes accessed | tf_op | source)
XLA Modules:
  0.0 53.9 jit_solution(4306743829022984880)
XLA Ops:
  0.6 51.6 %shard_map.129 = (bf16[128,256]{1,0:T(8,128)(2,1)}, bf16[128,128]{1,0:T(8,128)(2,1)}, f32[128,256]{1,0:T(8,128)}, f32[2,128]{1,0:T(2,128)}) custom-call(bf16[128,128]{1,0:T(8,128)(2,1)} %feat_hbm.1, bf16[128,256]{1,0:T(8,128)(2,1)} %weight_hbm.1, f32[1,256]{1,0:T(1,128)} %bitcast.3, s32[1,128]{1,0:T(1,128)} %bitcast.4, s32[8,1,384]{2,1,0:T(1,128)} %dst_hbm.1, ...), custom_call_target="tpu_custom_call" | custom-call | tf_op jit(solution)/shard_map/pallas_call | solution.py:399
  52.3 1.7 %shard_map.130 = (bf16[128,256]{1,0:T(8,128)(2,1)}, bf16[128,128]{1,0:T(8,128)(2,1)}, f32[128,256]{1,0:T(8,128)}, f32[2,128]{1,0:T(2,128)}) custom-call(bf16[128,256]{1,0:T(8,128)(2,1)} %get-tuple-element.12.act, bf16[128,128]{1,0:T(8,128)(2,1)} %get-tuple-element.13.gfeat, f32[128,256]{1,0:T(8,128)} %get-tuple-element.14.gw, f32[2,128]{1,0:T(2,128)} %get-tuple-element.15.gb), custom_call_target="tpu_custom_call" | custom-call | tf_op jit(solution)/shard_map/pallas_call | solution.py:451

commit v7 on v6

--- a/solution.py
+++ b/solution.py
@@ -197,9 +197,9 @@
 
     for i in (4, 3, 5, 2, 6, 1, 7):
         table_z(i).start()
-    line_sends(xrow, xs_send, xs_recv)
     for i in (2, 1, 3):
         table_y(i).start()
+    line_sends(xrow, xs_send, xs_recv)
     mid[c, z] = sendtab[z]
     ya[y] = loctab[y]
 
@@ -210,6 +210,11 @@
         return remote(psend.at[a], precv.at[blk], p_send, p_recv, dom, a)
 
     def local_part(i, carry):
+        @pl.when(i == 4)
+        def _():
+            taken(mid.at[c, pl.ds(0, ZN - 1)], i_send.at[0], i_recv.at[0]).wait_recv()
+            table_relay.start()
+
         a = mod(blk + 1 + i, NB)
         dst_hot = hot(dst_ref[a], ROWS)
         src_hot = hot(src_ref[a], ROWS)
@@ -231,8 +236,6 @@
 
     lax.fori_loop(0, NB, local_part, 0)
 
-    taken(mid.at[c, pl.ds(0, ZN - 1)], i_send.at[0], i_recv.at[0]).wait_recv()
-    table_relay.start()
     taken(ya.at[pl.ds(0, YH - 1)], i_send.at[1], i_recv.at[1]).wait_recv()
     remote(mid.at[1 - c], mid.at[1 - c], i_send.at[2], i_recv.at[2], dom, blk).wait_recv()
 

time: 54.1 us -> 53.7 us (level)
  no operation moved by 1% of the time
where the time goes in v7:
time: 53.7 us; the launch traced here: 53.5 us
  Pallas kernels  52.9 us (99%)
  between operations  0.64 us (1%)
    pallas_call x1, Pallas kernels, per_device(): pl.pallas_call(kernel, out_shape=shapes, in_specs=[hbm] * 10, out_specs=(...  51.2 us
    pallas_call x1, Pallas kernels, per_device(): pl.pallas_call(write_kernel, out_shape=shapes, in_specs=[hbm] * 4, out_sp...  1.66 us

profile of v7, /device:TPU:1, one launch (start us, length us, event | category | flops | bytes accessed | tf_op | source)
XLA Modules:
  0.0 53.5 jit_solution(12691433667501231244)
XLA Ops:
  0.6 51.2 %shard_map.129 = (bf16[128,256]{1,0:T(8,128)(2,1)}, bf16[128,128]{1,0:T(8,128)(2,1)}, f32[128,256]{1,0:T(8,128)}, f32[2,128]{1,0:T(2,128)}) custom-call(bf16[128,128]{1,0:T(8,128)(2,1)} %feat_hbm.1, bf16[128,256]{1,0:T(8,128)(2,1)} %weight_hbm.1, f32[1,256]{1,0:T(1,128)} %bitcast.3, s32[1,128]{1,0:T(1,128)} %bitcast.4, s32[8,1,384]{2,1,0:T(1,128)} %dst_hbm.1, ...), custom_call_target="tpu_custom_call" | custom-call | tf_op jit(solution)/shard_map/pallas_call | solution.py:402
  51.9 1.7 %shard_map.130 = (bf16[128,256]{1,0:T(8,128)(2,1)}, bf16[128,128]{1,0:T(8,128)(2,1)}, f32[128,256]{1,0:T(8,128)}, f32[2,128]{1,0:T(2,128)}) custom-call(bf16[128,256]{1,0:T(8,128)(2,1)} %get-tuple-element.12.act, bf16[128,128]{1,0:T(8,128)(2,1)} %get-tuple-element.13.gfeat, f32[128,256]{1,0:T(8,128)} %get-tuple-element.14.gw, f32[2,128]{1,0:T(2,128)} %get-tuple-element.15.gb), custom_call_target="tpu_custom_call" | custom-call | tf_op jit(solution)/shard_map/pallas_call | solution.py:454
